TPU v7x, 128 devices: a whole 4x4x4 slice. The times are simulated.
128 devices in a mesh: lat: 8 (over z, y_lo), lon: 16 (over x, y_hi, core).
Axes of the slice: x: 4, y: 4 (y_hi: 2, y_lo: 2; y = y_hi * 2 + y_lo), z: 4, core: 2. Of those that a mesh axis runs over, the one named last changes fastest.
Arguments:
- latent: bfloat16 [4, 96, 384, 512], P(None, 'lat', 'lon'), may hold values from -6 to 6
- gain_first: float32 [512], replicated, may hold values from 0.25 to 1.75
- triple_first: bfloat16 [512, 1536], replicated, may hold values from -3.75 to 3.75
- output_first: bfloat16 [512, 512], replicated, may hold values from -0.25 to 0.25
- gain_merge: float32 [2048], replicated, may hold values from 0.25 to 1.75
- merge_weight: bfloat16 [2048, 1024], replicated, may hold values from -0.125 to 0.125
- gain_second: float32 [1024], replicated, may hold values from 0.25 to 1.75
- triple_second: bfloat16 [1024, 3072], replicated, may hold values from -2.6516504 to 2.6516504
- output_second: bfloat16 [1024, 1024], replicated, may hold values from -0.1875 to 0.1875
- split_weight: bfloat16 [1024, 2048], replicated, may hold values from -0.1875 to 0.1875
Outputs:
- decoded: bfloat16 [4, 96, 384, 512], P(None, 'lat', 'lon')
- level_means: float32 [4, 512], replicated
All inputs are finite; a program needn't handle non-finite values.
Results may differ from a plain program's by a relative error of at most 0.028.
Values may be sent and summed in bfloat16 or wider, within the bound.
A program may use at most 192 MiB of HBM per device.

v0:
```python
import functools

import jax
import jax.numpy as jnp
import ml_dtypes
import numpy as np
from jax import lax
from jax.experimental import pallas as pl
from jax.experimental.pallas import tpu as pltpu
from jax.sharding import PartitionSpec as P

HD = 64
D1 = 512
D2 = 1024
EPS = 1e-05
MASKED = -1e30
QUAD = 72
WIN = 288
GROUP = 144
MESH = pl.DeviceIdType.MESH
F32 = jnp.float32
BF16 = jnp.bfloat16


def permutation(rows, source):
    matrix = np.zeros((rows, rows), np.float32)
    matrix[np.arange(rows), source] = 1.0
    return matrix.astype(ml_dtypes.bfloat16)


@functools.lru_cache(None)
def tables(lats, lons):
    q, l, r, c = np.meshgrid(*map(np.arange, (4, 4, 3, 6)), indexing="ij")
    to_quads = permutation(WIN, (l * 72 + r * 24 + q * 6 + c).ravel())
    p, q, r, c = np.meshgrid(*map(np.arange, (4, 4, 3, 6)), indexing="ij")
    to_window = permutation(WIN, (((q * 4 + (p + 1) % 4) * 3 + r) * 6 + c).ravel())
    ro, co, l, cr, cc = np.meshgrid(*map(np.arange, (2, 2, 4, 3, 6)), indexing="ij")
    row, col = 2 * cr + ro, 2 * cc + co
    quad = (row // 3) * 2 + col // 6
    to_patches = permutation(WIN, (((quad * 4 + l) * 3 + row % 3) * 6 + col % 6).ravel())
    l, row, col = np.meshgrid(*map(np.arange, (4, 6, 24)), indexing="ij")
    j, col = col // 12, col % 12
    off = (row % 2) * 2 + col % 2
    to_rows = permutation(
        2 * WIN, ((((j * 4 + off) * 4 + l) * 3 + row // 2) * 6 + col // 2).ravel()
    )
    total_rows = 12 * lats
    position = (np.arange(total_rows, dtype=np.float32) + np.float32(0.5)) / np.float32(
        total_rows
    ) - np.float32(0.5)
    weights = np.cos(np.float32(np.pi) * position).astype(np.float32)
    scale = float(np.sqrt(24.0 * lons * np.sum(weights.astype(np.float64) ** 2)))
    high = weights.astype(ml_dtypes.bfloat16)
    low = (weights - high.astype(np.float32)).astype(ml_dtypes.bfloat16)
    parts = np.stack([high, low]).astype(np.float32)
    sums = np.zeros((lats, 3, 16, WIN), np.float32)
    quad, l, r, c = [v.ravel() for v in np.meshgrid(*map(np.arange, (4, 4, 3, 6)), indexing="ij")]
    token = np.arange(WIN)
    for lat in range(lats):
        for part in range(2):
            for a in range(2):
                row = (lat * 12 + 3 + 6 * a + 3 * (quad // 2) + r) % total_rows
                sums[lat, a, part * 4 + l, token] = parts[part, row]
            for ro in range(2):
                row = (2 * (lat * 6 + 3 + 3 * (quad // 2) + r) + ro) % total_rows
                sums[lat, 2, part * 8 + ro * 4 + l, token] = parts[part, row]
    return (
        to_quads,
        to_window,
        np.ascontiguousarray(to_window.T),
        to_patches,
        to_rows,
        sums.astype(ml_dtypes.bfloat16),
        scale,
    )


def dot(a, b):
    return jnp.dot(a, b, preferred_element_type=F32)


def dot_nt(a, b):
    return lax.dot_general(a, b, (((1,), (1,)), ((), ())), preferred_element_type=F32)


def layer_norm(x, gain):
    mean = jnp.mean(x, -1, keepdims=True)
    centred = x - mean
    var = jnp.mean(centred * centred, -1, keepdims=True)
    return centred * lax.rsqrt(var + EPS) * gain


def kernel(
    lats,
    lons,
    scale,
    latent_h,
    triple1_h,
    out1_h,
    merge_h,
    triple2_h,
    out2_h,
    split_h,
    quads_h,
    window_h,
    unwindow_h,
    patches_h,
    rows_h,
    sums_h,
    gain1,
    gainm,
    gain2,
    decoded,
    means,
    latent,
    triple1,
    out1,
    mergew,
    triple2,
    out2,
    splitw,
    quads_p,
    window_p,
    unwindow_p,
    patches_p,
    rows_p,
    sums,
    xq,
    fq,
    normed,
    qs,
    ks,
    vs,
    att,
    bias,
    grouped,
    groupn,
    coarse,
    up,
    ur,
    ub,
    fg,
    fsum,
    part1,
    part2,
    load_sem,
    send_sem,
    recv_sem,
    ar_send,
    ar_recv,
):
    lat = lax.axis_index("lat")
    lon = lax.axis_index("lon")

    def at(dlat, dlon):
        return {
            "lat": lax.rem(lat + dlat + lats, lats),
            "lon": lax.rem(lon + dlon + lons, lons),
        }

    loads = [
        pltpu.make_async_copy(s, d, load_sem.at[i])
        for i, (s, d) in enumerate(
            [
                (latent_h, latent),
                (quads_h, quads_p),
                (window_h, window_p),
                (triple1_h, triple1),
                (unwindow_h, unwindow_p),
                (out1_h, out1),
                (sums_h.at[lat], sums),
                (patches_h, patches_p),
                (merge_h, mergew),
                (triple2_h, triple2),
                (out2_h, out2),
                (split_h, splitw),
                (rows_h, rows_p),
            ]
        )
    ]
    (l_latent, l_quads, l_window, l_triple1, l_unwindow, l_out1, l_sums) = loads[:7]
    (l_patches, l_merge, l_triple2, l_out2, l_split, l_rows) = loads[7:]
    for load in loads:
        load.start()

    barrier = pltpu.get_barrier_semaphore()
    peers = [at(k, 0) for k in range(1, lats)] + [at(0, k) for k in range(1, lons)]
    peers += [at(1, 1), at(-1, -1)]
    for peer in peers:
        pl.semaphore_signal(barrier, inc=1, device_id=peer, device_id_type=MESH)

    tq = lax.broadcasted_iota(jnp.int32, (GROUP, GROUP), 0)
    tk = lax.broadcasted_iota(jnp.int32, (GROUP, GROUP), 1)
    lev_q, lev_k = tq >= 72, tk >= 72
    half_q = jnp.where(lev_q, tq - 72, tq) >= 36
    half_k = jnp.where(lev_k, tk - 72, tk) >= 36
    other_lev = jnp.where(lev_q == lev_k, 0.0, MASKED).astype(F32)
    other_row = jnp.where(half_q == half_k, 0.0, MASKED).astype(F32)
    bias[0] = jnp.zeros((GROUP, GROUP), F32)
    bias[1] = other_lev
    bias[2] = other_row
    bias[3] = jnp.minimum(other_lev, other_row)
    fsum[...] = jnp.zeros_like(fsum)

    def copy(number, src, dst, target):
        return pltpu.make_async_remote_copy(
            src_ref=src,
            dst_ref=dst,
            send_sem=send_sem.at[number],
            recv_sem=recv_sem.at[number],
            device_id=target,
            device_id_type=MESH,
        )

    x_lat = copy(0, xq.at[0, pl.ds(1, 3)], xq.at[4, pl.ds(1, 3)], at(-1, 0))
    x_lon = copy(1, xq.at[pl.ds(1, 3), 0], xq.at[pl.ds(1, 3), 4], at(0, -1))
    x_dia = copy(2, xq.at[0, 0], xq.at[4, 4], at(-1, -1))
    f_lat = copy(3, fq.at[1, pl.ds(2, 3)], fq.at[5, pl.ds(2, 3)], at(-1, 0))
    f_lon = copy(4, fq.at[pl.ds(2, 3), 1], fq.at[pl.ds(2, 3), 5], at(0, -1))
    f_dia = copy(5, fq.at[1, 1], fq.at[5, 5], at(-1, -1))
    b_lat = copy(6, fq.at[4, pl.ds(1, 3)], fq.at[0, pl.ds(1, 3)], at(1, 0))
    b_lon = copy(7, fq.at[pl.ds(1, 3), 4], fq.at[pl.ds(1, 3), 0], at(0, 1))
    b_dia = copy(8, fq.at[4, 4], fq.at[0, 0], at(1, 1))
    u_lat = copy(9, up.at[1, 0], ur.at[0, 1], at(1, 0))
    u_lon = copy(10, up.at[0, 1], ur.at[1, 0], at(0, 1))
    u_dia = copy(11, up.at[1, 1], ur.at[0, 0], at(1, 1))

    l_latent.wait()
    l_quads.wait()

    def form_quads(qr, carry):
        rows = latent[:, qr].astype(F32).reshape(WIN, D1).astype(BF16)
        xq[qr, pl.ds(0, 4)] = dot(quads_p[...], rows).reshape(4, QUAD, D1).astype(BF16)
        return carry

    lax.fori_loop(0, 4, form_quads, 0)

    pl.semaphore_wait(barrier, len(peers))
    x_lon.start()
    x_lat.start()
    x_dia.start()

    l_window.wait()
    l_triple1.wait()
    l_unwindow.wait()
    l_out1.wait()
    l_sums.wait()

    lane = lax.broadcasted_iota(jnp.int32, (1, 256), 1)
    head_masks = [((lane >= HD * h) & (lane < HD * (h + 1))).astype(BF16) for h in range(4)]
    head_ones = [jnp.broadcast_to(m, (GROUP, 256)) for m in head_masks]

    def section(x, gain, triple, out_w, width, rows_apart):
        n = layer_norm(x, gain).astype(BF16)
        normed[:, :width] = dot(window_p[...], n).astype(BF16)
        groups = width // 256

        for which, dest in enumerate((qs, ks, vs)):

            def project(i, carry, which=which, dest=dest):
                src = pl.ds(pl.multiple_of(which * width + i * 256, 256), 256)
                dst = pl.ds(pl.multiple_of(i * 256, 256), 256)
                value = dot(normed[:, :width], triple[:, src]).astype(BF16)
                if which == 0:
                    value = value * jnp.asarray(HD**-0.5, BF16)
                dest[:, dst] = value
                return carry

            lax.fori_loop(0, groups, project, 0)

        def attend(i, carry):
            g, hg = i // groups, i % groups
            rows = pl.ds(pl.multiple_of(g * GROUP, 16), GROUP)
            lanes = pl.ds(pl.multiple_of(hg * 256, 256), 256)
            q, k, v = qs[rows, lanes], ks[rows, lanes], vs[rows, lanes]
            away = bias[g + 2 * rows_apart]
            total = None
            for h in range(4):
                s = dot_nt(q, k * head_masks[h]) + away
                peak = jnp.max(s, -1, keepdims=True)
                e = jnp.exp(s - peak).astype(BF16)
                top = dot(e, v * head_masks[h])
                low = dot(e, head_ones[h])
                total = (top, low) if total is None else (total[0] + top, total[1] + low)
            att[rows, lanes] = (total[0] / total[1]).astype(BF16)
            return carry

        lax.fori_loop(0, 2 * groups, attend, 0)
        back = dot(unwindow_p[...], att[:, :width]).astype(BF16)
        return x + dot(back, out_w[...])

    def fine_window(w, carry):
        a, b = w // 2, w % 2

        @pl.when(w == 1)
        def _():
            x_lon.wait_recv()

        @pl.when(w == 2)
        def _():
            x_lat.wait_recv()

        @pl.when(w == 3)
        def _():
            x_dia.wait_recv()

        quads_r, quads_c = pl.ds(1 + 2 * a, 2), pl.ds(1 + 2 * b, 2)
        x = xq[quads_r, quads_c].astype(F32).reshape(WIN, D1)
        apart = jnp.where((a == 1) & (lat == lats - 1), 1, 0)
        fine = section(x, gain1[...], triple1, out1, D1, apart)
        fq[quads_r, quads_c] = fine.reshape(2, 2, QUAD, D1).astype(BF16)
        fsum[...] += dot(sums[a], fine.astype(BF16))

        @pl.when(w == 0)
        def _():
            f_dia.start()

        @pl.when(w == 1)
        def _():
            f_lat.start()

        @pl.when(w == 2)
        def _():
            f_lon.start()

        return carry

    lax.fori_loop(0, 4, fine_window, 0)
    b_lon.start()
    b_lat.start()
    b_dia.start()

    l_patches.wait()

    def patches(first_r, first_c):
        x = fq[pl.ds(first_r, 2), pl.ds(first_c, 2)].astype(F32).reshape(WIN, D1).astype(BF16)
        return dot(patches_p[...], x)

    f_dia.wait_recv()
    f_lat.wait_recv()
    f_lon.wait_recv()

    def gather(cq, carry):
        x = patches(2 + 2 * (cq // 2), 2 + 2 * (cq % 2))
        rows = pl.ds(pl.multiple_of(cq * QUAD, 8), QUAD)
        for off in range(4):
            grouped[rows, off * D1 : (off + 1) * D1] = x[off * QUAD : (off + 1) * QUAD]
        return carry

    lax.fori_loop(0, 4, gather, 0)

    def norm_grouped(i, carry):
        rows = pl.ds(pl.multiple_of(i * 96, 16), 96)
        groupn[rows, :] = layer_norm(grouped[rows, :], gainm[...]).astype(BF16)
        return carry

    lax.fori_loop(0, 3, norm_grouped, 0)
    l_merge.wait()

    def merge(i, carry):
        lanes = pl.ds(pl.multiple_of(i * 256, 256), 256)
        coarse[:, lanes] = dot(groupn[...], mergew[:, lanes]).astype(BF16)
        return carry

    lax.fori_loop(0, 4, merge, 0)
    l_triple2.wait()
    l_out2.wait()
    apart = jnp.where(lat == lats - 1, 1, 0)
    upper = section(coarse[...].astype(F32), gain2[...], triple2, out2, D2, apart)
    up[...] = upper.reshape(2, 2, QUAD, D2).astype(BF16)
    u_lon.start()
    u_lat.start()
    u_dia.start()
    ur[1, 1] = up[0, 0]

    usum = dot(sums[2], upper.astype(BF16))
    usum = usum[:8] + usum[8:]
    high = usum.astype(BF16).astype(F32)
    usum = jnp.concatenate([high, usum - high], 0).astype(BF16)
    l_split.wait()
    partial = fsum[0:4] + fsum[4:8]
    for ro in range(2):
        for co in range(2):
            off = 2 * ro + co
            t = dot(usum, splitw[:, off * D1 : (off + 1) * D1])
            t = t[:8] + t[8:]
            partial += t[4 * ro : 4 * ro + 4]
    part1[lat] = partial

    def ar_copy(buf, me, number, target):
        return pltpu.make_async_remote_copy(
            src_ref=buf.at[me],
            dst_ref=buf.at[me],
            send_sem=ar_send.at[number],
            recv_sem=ar_recv.at[number],
            device_id=target,
            device_id_type=MESH,
        )

    ar1 = [ar_copy(part1, lat, k, at(k, 0)) for k in range(1, lats)]
    ar2 = [ar_copy(part2, lon, lats + k, at(0, k)) for k in range(1, lons)]
    for c in ar1:
        c.start()

    b_lat.wait_recv()
    b_lon.wait_recv()
    b_dia.wait_recv()

    def skip(cq, carry):
        x = patches(2 * (cq // 2), 2 * (cq % 2))
        rows = pl.ds(pl.multiple_of(cq * QUAD, 8), QUAD)
        for off in range(4):
            fg[off, rows, :] = x[off * QUAD : (off + 1) * QUAD]
        return carry

    lax.fori_loop(0, 4, skip, 0)

    for c in ar1:
        c.wait_recv()
    total = part1[0]
    for k in range(1, lats):
        total += part1[k]
    part2[lon] = total
    for c in ar2:
        c.start()

    u_lat.wait_recv()
    u_lon.wait_recv()
    u_dia.wait_recv()
    ub[...] = ur[...].astype(F32).reshape(WIN, D2).astype(BF16)

    def spread(i, carry):
        off, half = i // 2, i % 2
        src = pl.ds(pl.multiple_of(i * 256, 256), 256)
        dst = pl.ds(pl.multiple_of(half * 256, 256), 256)
        fg[off, :, dst] += dot(ub[...], splitw[:, src])
        return carry

    lax.fori_loop(0, 8, spread, 0)
    l_rows.wait()

    def place(i, carry):
        pieces = []
        for j in range(2):
            rows = pl.ds(pl.multiple_of((2 * i + j) * QUAD, 8), QUAD)
            for off in range(4):
                pieces.append(fg[off, rows, :])
        x = jnp.concatenate(pieces, 0).astype(BF16)
        decoded[:, i] = dot(rows_p[...], x).reshape(4, 144, D1).astype(BF16)
        return carry

    lax.fori_loop(0, 2, place, 0)

    for c in ar2:
        c.wait_recv()
    total = part2[0]
    for k in range(1, lons):
        total += part2[k]
    means[...] = total * (1.0 / scale)
    for c in (x_lat, x_lon, x_dia, f_lat, f_lon, f_dia, b_lat, b_lon, b_dia, u_lat, u_lon, u_dia):
        c.wait_send()
    for c in ar1 + ar2:
        c.wait_send()


def solution(mesh):
    lats, lons = mesh.shape["lat"], mesh.shape["lon"]
    *consts, scale = tables(lats, lons)

    def shards(
        latent,
        gain_first,
        triple_first,
        output_first,
        gain_merge,
        merge_weight,
        gain_second,
        triple_second,
        output_second,
        split_weight,
    ):
        hbm = pl.BlockSpec(memory_space=pl.ANY)
        vmem = pl.BlockSpec(memory_space=pltpu.VMEM)
        bf = lambda *shape: pltpu.VMEM(shape, BF16)
        f4 = lambda *shape: pltpu.VMEM(shape, F32)
        decoded, means = pl.pallas_call(
            functools.partial(kernel, lats, lons, scale),
            name="windows",
            out_shape=(
                jax.ShapeDtypeStruct((4, 2, 144, D1), BF16),
                jax.ShapeDtypeStruct((4, D1), F32),
            ),
            in_specs=[hbm] * 13 + [vmem] * 3,
            out_specs=(vmem, vmem),
            scratch_shapes=[
                bf(4, 4, QUAD, D1),
                bf(D1, 3 * D1),
                bf(D1, D1),
                bf(4 * D1, D2),
                bf(D2, 3 * D2),
                bf(D2, D2),
                bf(D2, 4 * D1),
                bf(WIN, WIN),
                bf(WIN, WIN),
                bf(WIN, WIN),
                bf(WIN, WIN),
                bf(2 * WIN, 2 * WIN),
                bf(3, 16, WIN),
                bf(5, 5, QUAD, D1),
                bf(6, 6, QUAD, D1),
                bf(WIN, D2),
                bf(WIN, D2),
                bf(WIN, D2),
                bf(WIN, D2),
                bf(WIN, D2),
                f4(4, GROUP, GROUP),
                f4(WIN, 4 * D1),
                bf(WIN, 4 * D1),
                bf(WIN, D2),
                bf(2, 2, QUAD, D2),
                bf(2, 2, QUAD, D2),
                bf(WIN, D2),
                f4(4, WIN, D1),
                f4(16, D1),
                f4(lats, 4, D1),
                f4(lons, 4, D1),
                pltpu.SemaphoreType.DMA((13,)),
                pltpu.SemaphoreType.DMA((12,)),
                pltpu.SemaphoreType.DMA((12,)),
                pltpu.SemaphoreType.DMA((lats + lons,)),
                pltpu.SemaphoreType.DMA((lats + lons,)),
            ],
            compiler_params=pltpu.CompilerParams(
                collective_id=0, has_side_effects=True, vmem_limit_bytes=60 * 1024 * 1024
            ),
        )(
            latent.reshape(4, 4, QUAD, D1),
            triple_first,
            output_first,
            merge_weight,
            triple_second,
            output_second,
            split_weight,
            *[jnp.asarray(c) for c in consts],
            gain_first.reshape(1, -1),
            gain_merge.reshape(1, -1),
            gain_second.reshape(1, -1),
        )
        return decoded.reshape(4, 12, 24, D1), means

    in_specs = (P(None, "lat", "lon", None),) + (P(),) * 9
    out_specs = (P(None, "lat", "lon", None), P())
    return jax.shard_map(
        shards, mesh=mesh, in_specs=in_specs, out_specs=out_specs, check_vma=False
    )
```

profile of v0, /device:TPU:1, one launch (start us, length us, event | category | flops | bytes accessed | tf_op | source)
XLA Modules:
  0.0 75.8 jit_solution(1719186620614332132)
XLA Ops:
  0.6 72.2 %windows.1 = (bf16[4,2,144,512]{3,2,1,0:T(8,128)(2,1)}, f32[4,512]{1,0:T(4,128)}) custom-call(bf16[4,4,72,512]{3,2,1,0:T(8,128)(2,1)} %bitcast.5, bf16[512,1536]{1,0:T(8,128)(2,1)} %triple1_h.1, bf16[512,512]{1,0:T(8,128)(2,1)} %out1_h.1, bf16[2048,1024]{1,0:T(8,128)(2,1)} %merge_h.1, bf16[1024,3072]{1,0:T(8,128)(2,1)} %triple2_h.1, ...), custom_call_target="tpu_custom_call" | custom-call | tf_op jit(solution)/shard_map/windows/pallas_call | solution.py:486
  72.8 0.0 copy-start
  72.8 2.4 %copy.20 = bf16[4,12,24,512]{3,2,1,0:T(8,128)(2,1)} copy(bf16[4,12,24,512]{3,2,1,0:T(8,128)(2,1)} %bitcast.6) | data formatting | bytes 2359296
  75.2 0.0 copy-done
  75.2 0.6 copy.21
Async XLA Ops:
  72.8 2.4 %copy-start = (f32[4,512]{1,0:T(4,128)S(1)}, f32[4,512]{1,0:T(4,128)}, u32[]{:S(2)}) copy-start(f32[4,512]{1,0:T(4,128)} %get-tuple-element.9) | copy-start | bytes 24580
where the time goes:
time: 76 us; the launch traced here: 75.8 us
  Pallas kernels  72.2 us (95%)
  local copies, waits for them, and re-layouts  2.99 us (4%)
    pallas_call x1, Pallas kernels, shards(): pl.pallas_call(functools.partial(kernel, lats, lons, scale), name='window...  72.2 us
    unnamed x4, local copies, waits for them, and re-layouts  2.99 us

commit v1 on v0

--- a/solution.py
+++ b/solution.py
@@ -233,7 +233,7 @@
         xq[qr, pl.ds(0, 4)] = dot(quads_p[...], rows).reshape(4, QUAD, D1).astype(BF16)
         return carry
 
-    lax.fori_loop(0, 4, form_quads, 0)
+    lax.fori_loop(0, 4, form_quads, 0, unroll=True)
 
     pl.semaphore_wait(barrier, len(peers))
     x_lon.start()
@@ -248,7 +248,6 @@
 
     lane = lax.broadcasted_iota(jnp.int32, (1, 256), 1)
     head_masks = [((lane >= HD * h) & (lane < HD * (h + 1))).astype(BF16) for h in range(4)]
-    head_ones = [jnp.broadcast_to(m, (GROUP, 256)) for m in head_masks]
 
     def section(x, gain, triple, out_w, width, rows_apart):
         n = layer_norm(x, gain).astype(BF16)
@@ -266,7 +265,7 @@
                 dest[:, dst] = value
                 return carry
 
-            lax.fori_loop(0, groups, project, 0)
+            lax.fori_loop(0, groups, project, 0, unroll=True)
 
         def attend(i, carry):
             g, hg = i // groups, i % groups
@@ -274,18 +273,22 @@
             lanes = pl.ds(pl.multiple_of(hg * 256, 256), 256)
             q, k, v = qs[rows, lanes], ks[rows, lanes], vs[rows, lanes]
             away = bias[g + 2 * rows_apart]
-            total = None
+            scores = dot_nt(jnp.concatenate([q * mask for mask in head_masks], 0), k)
+            weights = []
             for h in range(4):
-                s = dot_nt(q, k * head_masks[h]) + away
+                s = scores[h * GROUP : (h + 1) * GROUP] + away
                 peak = jnp.max(s, -1, keepdims=True)
-                e = jnp.exp(s - peak).astype(BF16)
-                top = dot(e, v * head_masks[h])
-                low = dot(e, head_ones[h])
-                total = (top, low) if total is None else (total[0] + top, total[1] + low)
-            att[rows, lanes] = (total[0] / total[1]).astype(BF16)
+                weights.append(jnp.exp(s - peak).astype(BF16))
+            weights = jnp.concatenate(weights, 0)
+            values = dot(weights, v) / jnp.sum(weights.astype(F32), -1, keepdims=True)
+            result = values[:GROUP]
+            for h in range(1, 4):
+                own = values[h * GROUP : (h + 1) * GROUP]
+                result = jnp.where(lane >= HD * h, own, result)
+            att[rows, lanes] = result.astype(BF16)
             return carry
 
-        lax.fori_loop(0, 2 * groups, attend, 0)
+        lax.fori_loop(0, 2 * groups, attend, 0, unroll=4)
         back = dot(unwindow_p[...], att[:, :width]).astype(BF16)
         return x + dot(back, out_w[...])
 
@@ -347,14 +350,14 @@
             grouped[rows, off * D1 : (off + 1) * D1] = x[off * QUAD : (off + 1) * QUAD]
         return carry
 
-    lax.fori_loop(0, 4, gather, 0)
+    lax.fori_loop(0, 4, gather, 0, unroll=True)
 
     def norm_grouped(i, carry):
         rows = pl.ds(pl.multiple_of(i * 96, 16), 96)
         groupn[rows, :] = layer_norm(grouped[rows, :], gainm[...]).astype(BF16)
         return carry
 
-    lax.fori_loop(0, 3, norm_grouped, 0)
+    lax.fori_loop(0, 3, norm_grouped, 0, unroll=True)
     l_merge.wait()
 
     def merge(i, carry):
@@ -362,7 +365,7 @@
         coarse[:, lanes] = dot(groupn[...], mergew[:, lanes]).astype(BF16)
         return carry
 
-    lax.fori_loop(0, 4, merge, 0)
+    lax.fori_loop(0, 4, merge, 0, unroll=True)
     l_triple2.wait()
     l_out2.wait()
     apart = jnp.where(lat == lats - 1, 1, 0)
@@ -413,7 +416,7 @@
             fg[off, rows, :] = x[off * QUAD : (off + 1) * QUAD]
         return carry
 
-    lax.fori_loop(0, 4, skip, 0)
+    lax.fori_loop(0, 4, skip, 0, unroll=True)
 
     for c in ar1:
         c.wait_recv()
@@ -436,7 +439,7 @@
         fg[off, :, dst] += dot(ub[...], splitw[:, src])
         return carry
 
-    lax.fori_loop(0, 8, spread, 0)
+    lax.fori_loop(0, 8, spread, 0, unroll=True)
     l_rows.wait()
 
     def place(i, carry):
@@ -449,7 +452,7 @@
         decoded[:, i] = dot(rows_p[...], x).reshape(4, 144, D1).astype(BF16)
         return carry
 
-    lax.fori_loop(0, 2, place, 0)
+    lax.fori_loop(0, 2, place, 0, unroll=True)
 
     for c in ar2:
         c.wait_recv()

time: 76 us -> 58.2 us (0.77)
  Pallas kernels: 72.2 us -> 54.4 us
    pallas_call x1, Pallas kernels: 72.2 us -> 54.4 us  [shards(): pl.pallas_call(functools.partial(kernel, lats, lons, scale), name='window...]
where the time goes in v1:
time: 58.2 us; the launch traced here: 58.1 us
  Pallas kernels  54.4 us (93%)
  local copies, waits for them, and re-layouts  2.99 us (5%)
  between operations  0.65 us (1%)
    pallas_call x1, Pallas kernels, shards(): pl.pallas_call(functools.partial(kernel, lats, lons, scale), name='window...  54.4 us
    unnamed x4, local copies, waits for them, and re-layouts  2.99 us

profile of v1, /device:TPU:1, one launch (start us, length us, event | category | flops | bytes accessed | tf_op | source)
XLA Modules:
  0.0 58.1 jit_solution(6216861839331937572)
XLA Ops:
  0.6 54.4 %windows.1 = (bf16[4,2,144,512]{3,2,1,0:T(8,128)(2,1)}, f32[4,512]{1,0:T(4,128)}) custom-call(bf16[4,4,72,512]{3,2,1,0:T(8,128)(2,1)} %bitcast.5, bf16[512,1536]{1,0:T(8,128)(2,1)} %triple1_h.1, bf16[512,512]{1,0:T(8,128)(2,1)} %out1_h.1, bf16[2048,1024]{1,0:T(8,128)(2,1)} %merge_h.1, bf16[1024,3072]{1,0:T(8,128)(2,1)} %triple2_h.1, ...), custom_call_target="tpu_custom_call" | custom-call | tf_op jit(solution)/shard_map/windows/pallas_call | solution.py:489
  55.1 0.0 copy-start
  55.1 2.4 %copy.20 = bf16[4,12,24,512]{3,2,1,0:T(8,128)(2,1)} copy(bf16[4,12,24,512]{3,2,1,0:T(8,128)(2,1)} %bitcast.6) | data formatting | bytes 2359296
  57.5 0.0 copy-done
  57.5 0.6 %copy.21 = f32[4,512]{1,0:T(4,128)} copy(f32[4,512]{1,0:T(4,128)S(1)} %copy-done) | data formatting | bytes 16384
Async XLA Ops:
  55.1 2.4 %copy-start = (f32[4,512]{1,0:T(4,128)S(1)}, f32[4,512]{1,0:T(4,128)}, u32[]{:S(2)}) copy-start(f32[4,512]{1,0:T(4,128)} %get-tuple-element.9) | copy-start | bytes 24580

commit v2 on v0

v2 whole, which is shorter than its diff:
```python
import functools

import jax
import jax.numpy as jnp
import ml_dtypes
import numpy as np
from jax import lax
from jax.experimental import pallas as pl
from jax.experimental.pallas import tpu as pltpu
from jax.sharding import PartitionSpec as P

HD = 64
D1 = 512
D2 = 1024
EPS = 1e-05
MASKED = -1e30
QUAD = 40
QUADS = 160
GROUP = 144
LEVELS = np.array([[1, 2], [3, 0]])
MESH = pl.DeviceIdType.MESH
F32 = jnp.float32
BF16 = jnp.bfloat16


def permutation(rows, columns, place, source):
    matrix = np.zeros((rows, columns), np.float32)
    matrix[place.ravel(), source.ravel()] = 1.0
    return matrix.astype(ml_dtypes.bfloat16)


def grid(*extents):
    return np.meshgrid(*map(np.arange, extents), indexing="ij")


@functools.lru_cache(None)
def tables(lats, lons):
    q, l, r, c = grid(4, 2, 3, 6)
    quads = q * QUAD + l * 18 + r * 6 + c
    to_quads = permutation(QUADS, GROUP, quads, l * 72 + r * 24 + q * 6 + c)
    to_window = permutation(GROUP, QUADS, l * 72 + q * 18 + r * 6 + c, quads)
    ro, co, l, cr, cc = grid(2, 2, 2, 3, 6)
    row, col = 2 * cr + ro, 2 * cc + co
    quad = (row // 3) * 2 + col // 6
    to_patches = permutation(
        QUADS,
        QUADS,
        (2 * ro + co) * QUAD + l * 18 + cr * 6 + cc,
        quad * QUAD + l * 18 + (row % 3) * 6 + col % 6,
    )
    l, row, col = grid(2, 6, 24)
    j, c12 = col // 12, col % 12
    off = (row % 2) * 2 + c12 % 2
    to_rows = permutation(
        2 * GROUP,
        2 * QUADS,
        l * 144 + row * 24 + col,
        (j * 4 + off) * QUAD + l * 18 + (row // 2) * 6 + c12 // 2,
    )
    total_rows = 12 * lats
    position = (np.arange(total_rows, dtype=np.float32) + np.float32(0.5)) / np.float32(
        total_rows
    ) - np.float32(0.5)
    weights = np.cos(np.float32(np.pi) * position).astype(np.float32)
    scale = float(np.sqrt(24.0 * lons * np.sum(weights.astype(np.float64) ** 2)))
    high = weights.astype(ml_dtypes.bfloat16)
    low = (weights - high.astype(np.float32)).astype(ml_dtypes.bfloat16)
    parts = np.stack([high, low]).astype(np.float32)
    sums = np.zeros((lats, 2, 3, 16, GROUP), np.float32)
    l, quad, r, c = [v.ravel() for v in grid(2, 4, 3, 6)]
    token = np.arange(GROUP)
    for lat in range(lats):
        for half in range(2):
            level = LEVELS[half][l]
            for part in range(2):
                for a in range(2):
                    row = (lat * 12 + 3 + 6 * a + 3 * (quad // 2) + r) % total_rows
                    sums[lat, half, a, part * 4 + level, token] = parts[part, row]
                for ro in range(2):
                    row = (2 * (lat * 6 + 3 + 3 * (quad // 2) + r) + ro) % total_rows
                    sums[lat, half, 2, part * 8 + ro * 4 + level, token] = parts[part, row]
    return (
        to_quads,
        to_window,
        np.ascontiguousarray(to_window.T),
        to_patches,
        to_rows,
        sums.astype(ml_dtypes.bfloat16),
        scale,
    )


def dot(a, b):
    return jnp.dot(a, b, preferred_element_type=F32)


def dot_nt(a, b):
    return lax.dot_general(a, b, (((1,), (1,)), ((), ())), preferred_element_type=F32)


def layer_norm(x, gain):
    mean = jnp.mean(x, -1, keepdims=True)
    centred = x - mean
    var = jnp.mean(centred * centred, -1, keepdims=True)
    return centred * lax.rsqrt(var + EPS) * gain


def kernel(
    lats,
    lons,
    scale,
    latent_h,
    triple1_h,
    out1_h,
    merge_h,
    triple2_h,
    out2_h,
    split_h,
    quads_h,
    window_h,
    unwindow_h,
    patches_h,
    rows_h,
    sums_h,
    gain1,
    gainm,
    gain2,
    decoded,
    means,
    latent,
    triple1,
    out1,
    mergew,
    triple2,
    out2,
    splitw,
    quads_p,
    window_p,
    unwindow_p,
    patches_p,
    rows_p,
    sums,
    xq,
    fq,
    normed,
    qs,
    ks,
    vs,
    att,
    bias,
    grouped,
    groupn,
    coarse,
    up,
    ur,
    ub,
    fg,
    fsum,
    usums,
    part1,
    part2,
    load_sem,
    send_sem,
    recv_sem,
    ar_send,
    ar_recv,
):
    lat = lax.axis_index("lat")
    lon = lax.axis_index("lon")

    def at(dlat, dlon):
        return {
            "lat": lax.rem(lat + dlat + lats, lats),
            "lon": lax.rem(lon + dlon + lons, lons),
        }

    loads = [
        pltpu.make_async_copy(s, d, load_sem.at[i])
        for i, (s, d) in enumerate(
            [
                (latent_h, latent),
                (quads_h, quads_p),
                (window_h, window_p),
                (triple1_h, triple1),
                (unwindow_h, unwindow_p),
                (out1_h, out1),
                (sums_h.at[lat], sums),
                (patches_h, patches_p),
                (merge_h, mergew),
                (triple2_h, triple2),
                (out2_h, out2),
                (split_h, splitw),
                (rows_h, rows_p),
            ]
        )
    ]
    (l_latent, l_quads, l_window, l_triple1, l_unwindow, l_out1, l_sums) = loads[:7]
    (l_patches, l_merge, l_triple2, l_out2, l_split, l_rows) = loads[7:]
    for load in loads:
        load.start()

    barrier = pltpu.get_barrier_semaphore()
    peers = [at(k, 0) for k in range(1, lats)] + [at(0, k) for k in range(1, lons)]
    peers += [at(1, 1), at(-1, -1)]
    for peer in peers:
        pl.semaphore_signal(barrier, inc=1, device_id=peer, device_id_type=MESH)

    tq = lax.broadcasted_iota(jnp.int32, (GROUP, GROUP), 0)
    tk = lax.broadcasted_iota(jnp.int32, (GROUP, GROUP), 1)
    lev_q, lev_k = tq >= 72, tk >= 72
    half_q = jnp.where(lev_q, tq - 72, tq) >= 36
    half_k = jnp.where(lev_k, tk - 72, tk) >= 36
    other_lev = jnp.where(lev_q == lev_k, 0.0, MASKED).astype(F32)
    other_row = jnp.where(half_q == half_k, 0.0, MASKED).astype(F32)
    bias[0] = jnp.zeros((GROUP, GROUP), F32)
    bias[1] = other_lev
    bias[2] = other_row
    bias[3] = jnp.minimum(other_lev, other_row)
    fsum[...] = jnp.zeros_like(fsum)
    usums[...] = jnp.zeros_like(usums)

    def copy(number, half, src, dst, target):
        number = number + 12 * half
        return pltpu.make_async_remote_copy(
            src_ref=src,
            dst_ref=dst,
            send_sem=send_sem.at[number],
            recv_sem=recv_sem.at[number],
            device_id=target,
            device_id_type=MESH,
        )

    three, edge = pl.ds(1, 3), pl.ds(2, 3)

    def x_lat(h):
        return copy(0, h, xq.at[h, 0, three], xq.at[h, 4, three], at(-1, 0))

    def x_lon(h):
        return copy(1, h, xq.at[h, three, 0], xq.at[h, three, 4], at(0, -1))

    def x_dia(h):
        return copy(2, h, xq.at[h, 0, 0], xq.at[h, 4, 4], at(-1, -1))

    def f_lat(h):
        return copy(3, h, fq.at[h, 1, edge], fq.at[h, 5, edge], at(-1, 0))

    def f_lon(h):
        return copy(4, h, fq.at[h, edge, 1], fq.at[h, edge, 5], at(0, -1))

    def f_dia(h):
        return copy(5, h, fq.at[h, 1, 1], fq.at[h, 5, 5], at(-1, -1))

    def b_lat(h):
        return copy(6, h, fq.at[h, 4, three], fq.at[h, 0, three], at(1, 0))

    def b_lon(h):
        return copy(7, h, fq.at[h, three, 4], fq.at[h, three, 0], at(0, 1))

    def b_dia(h):
        return copy(8, h, fq.at[h, 4, 4], fq.at[h, 0, 0], at(1, 1))

    def u_lat(h):
        return copy(9, h, up.at[h, 1, 0], ur.at[h, 0, 1], at(1, 0))

    def u_lon(h):
        return copy(10, h, up.at[h, 0, 1], ur.at[h, 1, 0], at(0, 1))

    def u_dia(h):
        return copy(11, h, up.at[h, 1, 1], ur.at[h, 0, 0], at(1, 1))

    l_latent.wait()
    l_quads.wait()

    def form_quads(h):
        def form(qr, carry):
            rows = jnp.concatenate([latent[int(l), qr].astype(F32) for l in LEVELS[h]], 0)
            quads = dot(quads_p[...], rows.astype(BF16))
            xq[h, qr, pl.ds(0, 4)] = quads.reshape(4, QUAD, D1).astype(BF16)
            return carry

        lax.fori_loop(0, 4, form, 0, unroll=True)

    form_quads(0)
    pl.semaphore_wait(barrier, len(peers))
    x_lon(0).start()
    x_lat(0).start()
    x_dia(0).start()
    form_quads(1)
    x_lon(1).start()
    x_lat(1).start()
    x_dia(1).start()

    l_window.wait()
    l_triple1.wait()
    l_unwindow.wait()
    l_out1.wait()
    l_sums.wait()

    lane = lax.broadcasted_iota(jnp.int32, (1, 256), 1)
    head_masks = [((lane >= HD * h) & (lane < HD * (h + 1))).astype(BF16) for h in range(4)]

    def section(x, gain, triple, out_w, width, kinds):
        count = len(kinds)
        size = count * GROUP
        normed[:size, :width] = layer_norm(x, gain).astype(BF16)
        groups = width // 256

        for which, dest in enumerate((qs, ks, vs)):

            def project(i, carry, which=which, dest=dest):
                src = pl.ds(pl.multiple_of(which * width + i * 256, 256), 256)
                dst = pl.ds(pl.multiple_of(i * 256, 256), 256)
                value = dot(normed[:size, :width], triple[:, src]).astype(BF16)
                if which == 0:
                    value = value * jnp.asarray(HD**-0.5, BF16)
                dest[:size, dst] = value
                return carry

            lax.fori_loop(0, groups, project, 0, unroll=True)

        for slot in range(count):
            for hg in range(groups):
                rows = slice(slot * GROUP, (slot + 1) * GROUP)
                lanes = slice(hg * 256, (hg + 1) * 256)
                q, k, v = qs[rows, lanes], ks[rows, lanes], vs[rows, lanes]
                away = bias[kinds[slot]]
                scores = dot_nt(jnp.concatenate([q * mask for mask in head_masks], 0), k)
                weights = []
                for h in range(4):
                    s = scores[h * GROUP : (h + 1) * GROUP] + away
                    peak = jnp.max(s, -1, keepdims=True)
                    weights.append(jnp.exp(s - peak).astype(BF16))
                weights = jnp.concatenate(weights, 0)
                values = dot(weights, v) / jnp.sum(weights.astype(F32), -1, keepdims=True)
                result = values[:GROUP]
                for h in range(1, 4):
                    own = values[h * GROUP : (h + 1) * GROUP]
                    result = jnp.where(lane >= HD * h, own, result)
                att[rows, lanes] = result.astype(BF16)
        return x + dot(att[:size, :width], out_w[...])

    def fine_step(w, carry):
        pick = lambda yes: jnp.where(yes, 1, 0)
        slots = [
            (pick(w == 2), pick(w == 3), pick(w >= 1)),
            (pick(w != 1), pick(w >= 1), pick(w == 3)),
        ]

        @pl.when(w == 1)
        def _():
            x_lon(0).wait_recv()
            x_lat(0).wait_recv()

        @pl.when(w == 2)
        def _():
            x_lon(1).wait_recv()
            x_lat(1).wait_recv()

        @pl.when(w == 3)
        def _():
            x_dia(0).wait_recv()
            x_dia(1).wait_recv()

        x, kinds = [], []
        for h, a, b in slots:
            quads = xq[h, pl.ds(1 + 2 * a, 2), pl.ds(1 + 2 * b, 2)]
            x.append(dot(window_p[...], quads.astype(F32).reshape(QUADS, D1).astype(BF16)))
            kinds.append(h + jnp.where((a == 1) & (lat == lats - 1), 2, 0))
        fine = section(jnp.concatenate(x, 0), gain1[...], triple1, out1, D1, kinds).astype(BF16)
        for slot, (h, a, b) in enumerate(slots):
            own = fine[slot * GROUP : (slot + 1) * GROUP]
            quads = dot(unwindow_p[...], own).reshape(2, 2, QUAD, D1)
            fq[h, pl.ds(1 + 2 * a, 2), pl.ds(1 + 2 * b, 2)] = quads.astype(BF16)
            fsum[...] += dot(sums[h, a], own)

        @pl.when(w == 0)
        def _():
            f_dia(0).start()
            f_dia(1).start()

        @pl.when(w == 1)
        def _():
            f_lon(0).start()
            f_lat(0).start()

        @pl.when(w == 2)
        def _():
            f_lon(1).start()
            f_lat(1).start()

        return carry

    lax.fori_loop(0, 4, fine_step, 0)
    for h in range(2):
        b_lon(h).start()
        b_lat(h).start()
        b_dia(h).start()

    l_patches.wait()
    l_merge.wait()
    l_triple2.wait()
    l_out2.wait()

    def patches(h, first_r, first_c):
        x = fq[h, pl.ds(first_r, 2), pl.ds(first_c, 2)]
        return dot(patches_p[...], x.astype(F32).reshape(QUADS, D1).astype(BF16))

    def coarse_half(h, carry):
        f_dia(h).wait_recv()
        f_lat(h).wait_recv()
        f_lon(h).wait_recv()
        for cq in range(4):
            x = patches(h, 2 + 2 * (cq // 2), 2 + 2 * (cq % 2))
            for off in range(4):
                rows = slice(cq * QUAD, (cq + 1) * QUAD)
                grouped[rows, off * D1 : (off + 1) * D1] = x[off * QUAD : (off + 1) * QUAD]
        for i in range(2):
            rows = slice(i * 80, (i + 1) * 80)
            groupn[rows, :] = layer_norm(grouped[rows, :], gainm[...]).astype(BF16)
        for i in range(4):
            lanes = slice(i * 256, (i + 1) * 256)
            coarse[:, lanes] = dot(groupn[...], mergew[:, lanes]).astype(BF16)
        x = dot(window_p[...], coarse[...])
        kind = h + jnp.where(lat == lats - 1, 2, 0)
        upper = section(x, gain2[...], triple2, out2, D2, [kind]).astype(BF16)
        up[h] = dot(unwindow_p[...], upper).reshape(2, 2, QUAD, D2).astype(BF16)
        u_lon(h).start()
        u_lat(h).start()
        u_dia(h).start()
        ur[h, 1, 1] = up[h, 0, 0]
        usums[...] += dot(sums[h, 2], upper)
        return carry

    lax.fori_loop(0, 2, coarse_half, 0)

    usum = usums[:8] + usums[8:]
    high = usum.astype(BF16).astype(F32)
    usum = jnp.concatenate([high, usum - high], 0).astype(BF16)
    l_split.wait()
    partial = fsum[0:4] + fsum[4:8]
    for ro in range(2):
        for co in range(2):
            off = 2 * ro + co
            t = dot(usum, splitw[:, off * D1 : (off + 1) * D1])
            t = t[:8] + t[8:]
            partial += t[4 * ro : 4 * ro + 4]
    part1[lat] = partial

    def ar_copy(buf, me, number, target):
        return pltpu.make_async_remote_copy(
            src_ref=buf.at[me],
            dst_ref=buf.at[me],
            send_sem=ar_send.at[number],
            recv_sem=ar_recv.at[number],
            device_id=target,
            device_id_type=MESH,
        )

    ar1 = [ar_copy(part1, lat, k, at(k, 0)) for k in range(1, lats)]
    ar2 = [ar_copy(part2, lon, lats + k, at(0, k)) for k in range(1, lons)]
    for c in ar1:
        c.start()

    def skip(h):
        b_lat(h).wait_recv()
        b_lon(h).wait_recv()
        b_dia(h).wait_recv()
        for cq in range(4):
            x = patches(h, 2 * (cq // 2), 2 * (cq % 2))
            for off in range(4):
                rows = slice(cq * QUAD, (cq + 1) * QUAD)
                fg[h, off, rows, :] = x[off * QUAD : (off + 1) * QUAD]

    def split(h):
        u_lat(h).wait_recv()
        u_lon(h).wait_recv()
        u_dia(h).wait_recv()
        ub[...] = ur[h].astype(F32).reshape(QUADS, D2).astype(BF16)
        for i in range(8):
            dst = slice((i % 2) * 256, (i % 2) * 256 + 256)
            fg[h, i // 2, :, dst] += dot(ub[...], splitw[:, i * 256 : (i + 1) * 256])
        for i in range(2):
            pieces = []
            for j in range(2):
                rows = slice((2 * i + j) * QUAD, (2 * i + j + 1) * QUAD)
                pieces += [fg[h, off, rows, :] for off in range(4)]
            x = jnp.concatenate(pieces, 0).astype(BF16)
            x = dot(rows_p[...], x).astype(BF16)
            for l in range(2):
                decoded[int(LEVELS[h][l]), i] = x[l * 144 : (l + 1) * 144]

    skip(0)
    l_rows.wait()
    split(0)
    for c in ar1:
        c.wait_recv()
    total = part1[0]
    for k in range(1, lats):
        total += part1[k]
    part2[lon] = total
    for c in ar2:
        c.start()
    skip(1)
    split(1)

    for c in ar2:
        c.wait_recv()
    total = part2[0]
    for k in range(1, lons):
        total += part2[k]
    means[...] = total * (1.0 / scale)
    for c in (x_lat, x_lon, x_dia, f_lat, f_lon, f_dia, b_lat, b_lon, b_dia, u_lat, u_lon, u_dia):
        c(0).wait_send()
        c(1).wait_send()
    for c in ar1 + ar2:
        c.wait_send()


def solution(mesh):
    lats, lons = mesh.shape["lat"], mesh.shape["lon"]
    *consts, scale = tables(lats, lons)

    def shards(
        latent,
        gain_first,
        triple_first,
        output_first,
        gain_merge,
        merge_weight,
        gain_second,
        triple_second,
        output_second,
        split_weight,
    ):
        hbm = pl.BlockSpec(memory_space=pl.ANY)
        vmem = pl.BlockSpec(memory_space=pltpu.VMEM)
        bf = lambda *shape: pltpu.VMEM(shape, BF16)
        f4 = lambda *shape: pltpu.VMEM(shape, F32)
        decoded, means = pl.pallas_call(
            functools.partial(kernel, lats, lons, scale),
            name="windows",
            out_shape=(
                jax.ShapeDtypeStruct((4, 2, 144, D1), BF16),
                jax.ShapeDtypeStruct((4, D1), F32),
            ),
            in_specs=[hbm] * 13 + [vmem] * 3,
            out_specs=(vmem, vmem),
            scratch_shapes=[
                bf(4, 4, 72, D1),
                bf(D1, 3 * D1),
                bf(D1, D1),
                bf(4 * D1, D2),
                bf(D2, 3 * D2),
                bf(D2, D2),
                bf(D2, 4 * D1),
                bf(QUADS, GROUP),
                bf(GROUP, QUADS),
                bf(QUADS, GROUP),
                bf(QUADS, QUADS),
                bf(2 * GROUP, 2 * QUADS),
                bf(2, 3, 16, GROUP),
                bf(2, 5, 5, QUAD, D1),
                bf(2, 6, 6, QUAD, D1),
                bf(2 * GROUP, D2),
                bf(2 * GROUP, D2),
                bf(2 * GROUP, D2),
                bf(2 * GROUP, D2),
                bf(2 * GROUP, D2),
                f4(4, GROUP, GROUP),
                f4(QUADS, 4 * D1),
                bf(QUADS, 4 * D1),
                bf(QUADS, D2),
                bf(2, 2, 2, QUAD, D2),
                bf(2, 2, 2, QUAD, D2),
                bf(QUADS, D2),
                f4(2, 4, QUADS, D1),
                f4(16, D1),
                f4(16, D2),
                f4(lats, 4, D1),
                f4(lons, 4, D1),
                pltpu.SemaphoreType.DMA((13,)),
                pltpu.SemaphoreType.DMA((24,)),
                pltpu.SemaphoreType.DMA((24,)),
                pltpu.SemaphoreType.DMA((lats + lons,)),
                pltpu.SemaphoreType.DMA((lats + lons,)),
            ],
            compiler_params=pltpu.CompilerParams(
                collective_id=0, has_side_effects=True, vmem_limit_bytes=60 * 1024 * 1024
            ),
        )(
            latent.reshape(4, 4, 72, D1),
            triple_first,
            output_first,
            merge_weight,
            triple_second,
            output_second,
            split_weight,
            *[jnp.asarray(c) for c in consts],
            gain_first.reshape(1, -1),
            gain_merge.reshape(1, -1),
            gain_second.reshape(1, -1),
        )
        return decoded.reshape(4, 12, 24, D1), means

    in_specs = (P(None, "lat", "lon", None),) + (P(),) * 9
    out_specs = (P(None, "lat", "lon", None), P())
    return jax.shard_map(
        shards, mesh=mesh, in_specs=in_specs, out_specs=out_specs, check_vma=False
    )
```

time: 76 us -> 60.5 us (0.80)
  Pallas kernels: 72.2 us -> 56.7 us
    pallas_call x1, Pallas kernels: 72.2 us -> 56.7 us  [shards(): pl.pallas_call(functools.partial(kernel, lats, lons, scale), name='window...]
where the time goes in v2:
time: 60.5 us; the launch traced here: 60.3 us
  Pallas kernels  56.7 us (94%)
  local copies, waits for them, and re-layouts  2.99 us (5%)
  between operations  0.65 us (1%)
    pallas_call x1, Pallas kernels, shards(): pl.pallas_call(functools.partial(kernel, lats, lons, scale), name='window...  56.7 us
    unnamed x4, local copies, waits for them, and re-layouts  2.99 us

profile of v2, /device:TPU:1, one launch (start us, length us, event | category | flops | bytes accessed | tf_op | source)
XLA Modules:
  0.0 60.3 jit_solution(537428417944241657)
XLA Ops:
  0.6 56.7 %windows.1 = (bf16[4,2,144,512]{3,2,1,0:T(8,128)(2,1)}, f32[4,512]{1,0:T(4,128)}) custom-call(bf16[4,4,72,512]{3,2,1,0:T(8,128)(2,1)} %bitcast.5, bf16[512,1536]{1,0:T(8,128)(2,1)} %triple1_h.1, bf16[512,512]{1,0:T(8,128)(2,1)} %out1_h.1, bf16[2048,1024]{1,0:T(8,128)(2,1)} %merge_h.1, bf16[1024,3072]{1,0:T(8,128)(2,1)} %triple2_h.1, ...), custom_call_target="tpu_custom_call" | custom-call | tf_op jit(solution)/shard_map/windows/pallas_call | solution.py:539
  57.3 0.0 copy-start
  57.3 2.4 %copy.20 = bf16[4,12,24,512]{3,2,1,0:T(8,128)(2,1)} copy(bf16[4,12,24,512]{3,2,1,0:T(8,128)(2,1)} %bitcast.6) | data formatting | bytes 2359296
  59.7 0.0 copy-done
  59.7 0.6 copy.21
Async XLA Ops:
  57.3 2.4 %copy-start = (f32[4,512]{1,0:T(4,128)S(1)}, f32[4,512]{1,0:T(4,128)}, u32[]{:S(2)}) copy-start(f32[4,512]{1,0:T(4,128)} %get-tuple-element.9) | copy-start | bytes 24580

commit v3 on v2

--- a/solution.py
+++ b/solution.py
@@ -84,8 +84,8 @@
         to_window,
         np.ascontiguousarray(to_window.T),
         to_patches,
+        sums.astype(ml_dtypes.bfloat16),
         to_rows,
-        sums.astype(ml_dtypes.bfloat16),
         scale,
     )
 
@@ -120,12 +120,11 @@
     window_h,
     unwindow_h,
     patches_h,
-    rows_h,
     sums_h,
     gain1,
     gainm,
     gain2,
-    decoded,
+    pieces_h,
     means,
     latent,
     triple1,
@@ -138,7 +137,6 @@
     window_p,
     unwindow_p,
     patches_p,
-    rows_p,
     sums,
     xq,
     fq,
@@ -157,6 +155,7 @@
     fg,
     fsum,
     usums,
+    pieces_v,
     part1,
     part2,
     load_sem,
@@ -190,12 +189,11 @@
                 (triple2_h, triple2),
                 (out2_h, out2),
                 (split_h, splitw),
-                (rows_h, rows_p),
             ]
         )
     ]
     (l_latent, l_quads, l_window, l_triple1, l_unwindow, l_out1, l_sums) = loads[:7]
-    (l_patches, l_merge, l_triple2, l_out2, l_split, l_rows) = loads[7:]
+    (l_patches, l_merge, l_triple2, l_out2, l_split) = loads[7:]
     for load in loads:
         load.start()
 
@@ -424,9 +422,13 @@
         kind = h + jnp.where(lat == lats - 1, 2, 0)
         upper = section(x, gain2[...], triple2, out2, D2, [kind]).astype(BF16)
         up[h] = dot(unwindow_p[...], upper).reshape(2, 2, QUAD, D2).astype(BF16)
-        u_lon(h).start()
-        u_lat(h).start()
-        u_dia(h).start()
+
+        @pl.when(h == 0)
+        def _():
+            u_lon(0).start()
+            u_lat(0).start()
+            u_dia(0).start()
+
         ur[h, 1, 1] = up[h, 0, 0]
         usums[...] += dot(sums[h, 2], upper)
         return carry
@@ -460,6 +462,9 @@
     ar2 = [ar_copy(part2, lon, lats + k, at(0, k)) for k in range(1, lons)]
     for c in ar1:
         c.start()
+    u_lon(1).start()
+    u_lat(1).start()
+    u_dia(1).start()
 
     def skip(h):
         b_lat(h).wait_recv()
@@ -470,6 +475,9 @@
             for off in range(4):
                 rows = slice(cq * QUAD, (cq + 1) * QUAD)
                 fg[h, off, rows, :] = x[off * QUAD : (off + 1) * QUAD]
+
+    def out_copy(h, i):
+        return pltpu.make_async_copy(pieces_v.at[h, i], pieces_h.at[h, i], load_sem.at[12 + 2 * h + i])
 
     def split(h):
         u_lat(h).wait_recv()
@@ -484,13 +492,10 @@
             for j in range(2):
                 rows = slice((2 * i + j) * QUAD, (2 * i + j + 1) * QUAD)
                 pieces += [fg[h, off, rows, :] for off in range(4)]
-            x = jnp.concatenate(pieces, 0).astype(BF16)
-            x = dot(rows_p[...], x).astype(BF16)
-            for l in range(2):
-                decoded[int(LEVELS[h][l]), i] = x[l * 144 : (l + 1) * 144]
+            pieces_v[h, i] = jnp.concatenate(pieces, 0).astype(BF16)
+            out_copy(h, i).start()
 
     skip(0)
-    l_rows.wait()
     split(0)
     for c in ar1:
         c.wait_recv()
@@ -512,13 +517,42 @@
     for c in (x_lat, x_lon, x_dia, f_lat, f_lon, f_dia, b_lat, b_lon, b_dia, u_lat, u_lon, u_dia):
         c(0).wait_send()
         c(1).wait_send()
+    for h in range(2):
+        for i in range(2):
+            out_copy(h, i).wait()
     for c in ar1 + ar2:
         c.wait_send()
 
 
+def place(pieces_h, rows_p, means_in, decoded_h, means, pieces, decoded, in_sem, out_sem):
+    steps = [(h, i) for h in range(2) for i in range(2)]
+    loads = [
+        pltpu.make_async_copy(pieces_h.at[h, i], pieces.at[h, i], in_sem.at[n])
+        for n, (h, i) in enumerate(steps)
+    ]
+    for load in loads:
+        load.start()
+    means[...] = means_in[...]
+    stores = []
+    for n, (h, i) in enumerate(steps):
+        loads[n].wait()
+        x = dot(rows_p[...], pieces[h, i]).astype(BF16)
+        for l in range(2):
+            level = int(LEVELS[h][l])
+            decoded[level, i] = x[l * 144 : (l + 1) * 144]
+            stores.append(
+                pltpu.make_async_copy(
+                    decoded.at[level, i], decoded_h.at[level, i], out_sem.at[2 * n + l]
+                )
+            )
+            stores[-1].start()
+    for store in stores:
+        store.wait()
+
+
 def solution(mesh):
     lats, lons = mesh.shape["lat"], mesh.shape["lon"]
-    *consts, scale = tables(lats, lons)
+    *consts, to_rows, scale = tables(lats, lons)
 
     def shards(
         latent,
@@ -536,15 +570,15 @@
         vmem = pl.BlockSpec(memory_space=pltpu.VMEM)
         bf = lambda *shape: pltpu.VMEM(shape, BF16)
         f4 = lambda *shape: pltpu.VMEM(shape, F32)
-        decoded, means = pl.pallas_call(
+        pieces, means = pl.pallas_call(
             functools.partial(kernel, lats, lons, scale),
             name="windows",
             out_shape=(
-                jax.ShapeDtypeStruct((4, 2, 144, D1), BF16),
+                jax.ShapeDtypeStruct((2, 2, 2 * QUADS, D1), BF16),
                 jax.ShapeDtypeStruct((4, D1), F32),
             ),
-            in_specs=[hbm] * 13 + [vmem] * 3,
-            out_specs=(vmem, vmem),
+            in_specs=[hbm] * 12 + [vmem] * 3,
+            out_specs=(hbm, vmem),
             scratch_shapes=[
                 bf(4, 4, 72, D1),
                 bf(D1, 3 * D1),
@@ -557,7 +591,6 @@
                 bf(GROUP, QUADS),
                 bf(QUADS, GROUP),
                 bf(QUADS, QUADS),
-                bf(2 * GROUP, 2 * QUADS),
                 bf(2, 3, 16, GROUP),
                 bf(2, 5, 5, QUAD, D1),
                 bf(2, 6, 6, QUAD, D1),
@@ -576,9 +609,10 @@
                 f4(2, 4, QUADS, D1),
                 f4(16, D1),
                 f4(16, D2),
+                bf(2, 2, 2 * QUADS, D1),
                 f4(lats, 4, D1),
                 f4(lons, 4, D1),
-                pltpu.SemaphoreType.DMA((13,)),
+                pltpu.SemaphoreType.DMA((16,)),
                 pltpu.SemaphoreType.DMA((24,)),
                 pltpu.SemaphoreType.DMA((24,)),
                 pltpu.SemaphoreType.DMA((lats + lons,)),
@@ -600,6 +634,26 @@
             gain_merge.reshape(1, -1),
             gain_second.reshape(1, -1),
         )
+        decoded, means = pl.pallas_call(
+            place,
+            name="place",
+            out_shape=(
+                jax.ShapeDtypeStruct((4, 2, 144, D1), BF16),
+                jax.ShapeDtypeStruct((4, D1), F32),
+            ),
+            in_specs=[hbm, vmem, vmem],
+            out_specs=(hbm, vmem),
+            scratch_shapes=[
+                bf(2, 2, 2 * QUADS, D1),
+                bf(4, 2, 144, D1),
+                pltpu.SemaphoreType.DMA((4,)),
+                pltpu.SemaphoreType.DMA((8,)),
+            ],
+            cost_estimate=pl.CostEstimate(
+                flops=2 * 8 * 144 * 320 * D1, bytes_accessed=4000000, transcendentals=0
+            ),
+            compiler_params=pltpu.CompilerParams(vmem_limit_bytes=16 * 1024 * 1024),
+        )(pieces, jnp.asarray(to_rows), means)
         return decoded.reshape(4, 12, 24, D1), means
 
     in_specs = (P(None, "lat", "lon", None),) + (P(),) * 9

time: 60.5 us -> 60.7 us (level)
  Pallas kernels: 56.7 us -> 57.9 us
  local copies, waits for them, and re-layouts: 2.99 us -> 2.01 us
    pallas_call x0 -> x1, Pallas kernels: none -> 3.04 us  [shards(): pl.pallas_call(place, name='place', out_shape=(jax.ShapeDtypeStruct((4, 2...]
    pallas_call x1, Pallas kernels: 56.7 us -> 54.8 us  [shards(): pl.pallas_call(functools.partial(kernel, lats, lons, scale), name='window...]
    unnamed x4 -> x6, local copies, waits for them, and re-layouts: 2.99 us -> 2.01 us
where the time goes in v3:
time: 60.7 us; the launch traced here: 60.5 us
  Pallas kernels  57.9 us (95%)
  local copies, waits for them, and re-layouts  2.01 us (3%)
  between operations  0.67 us (1%)
    pallas_call x1, Pallas kernels, shards(): pl.pallas_call(functools.partial(kernel, lats, lons, scale), name='window...  54.8 us
    pallas_call x1, Pallas kernels, shards(): pl.pallas_call(place, name='place', out_shape=(jax.ShapeDtypeStruct((4, 2...  3.04 us
    unnamed x6, local copies, waits for them, and re-layouts  2.01 us

profile of v3, /device:TPU:1, one launch (start us, length us, event | category | flops | bytes accessed | tf_op | source)
XLA Modules:
  0.0 60.5 jit_solution(17026828132349600537)
XLA Ops:
  0.6 0.0 copy-start.1
  0.6 54.8 %windows.1 = (bf16[2,2,320,512]{3,2,1,0:T(8,128)(2,1)}, f32[4,512]{1,0:T(4,128)}) custom-call(bf16[4,4,72,512]{3,2,1,0:T(8,128)(2,1)} %bitcast.5, bf16[512,1536]{1,0:T(8,128)(2,1)} %triple1_h.1, bf16[512,512]{1,0:T(8,128)(2,1)} %out1_h.1, bf16[2048,1024]{1,0:T(8,128)(2,1)} %merge_h.1, bf16[1024,3072]{1,0:T(8,128)(2,1)} %triple2_h.1, ...), custom_call_target="tpu_custom_call" | custom-call | tf_op jit(solution)/shard_map/windows/pallas_call | solution.py:573
  55.5 0.0 copy-done.1
  55.5 0.0 copy-start
  55.5 1.3 %copy-done = bf16[2,2,320,512]{3,2,1,0:T(8,128)(2,1)S(1)} copy-done((bf16[2,2,320,512]{3,2,1,0:T(8,128)(2,1)S(1)}, bf16[2,2,320,512]{3,2,1,0:T(8,128)(2,1)}, u32[]{:S(2)}) %copy-start) | copy-done | bytes 1310744
  56.8 0.0 copy-start.2
  56.8 0.7 %copy-done.2 = f32[4,512]{1,0:T(4,128)S(1)} copy-done((f32[4,512]{1,0:T(4,128)S(1)}, f32[4,512]{1,0:T(4,128)}, u32[]{:S(2)}) %copy-start.2) | copy-done | bytes 8216
  57.5 3.0 %place.1 = (bf16[4,2,144,512]{3,2,1,0:T(8,128)(2,1)}, f32[4,512]{1,0:T(4,128)}) custom-call(bf16[2,2,320,512]{3,2,1,0:T(8,128)(2,1)S(1)} %copy-done, bf16[288,320]{1,0:T(8,128)(2,1)S(1)} %copy-done.1, f32[4,512]{1,0:T(4,128)S(1)} %copy-done.2), custom_call_target="tpu_custom_call" | custom-call | flops 377487360 | bytes 4000000 | tf_op jit(solution)/shard_map/place/pallas_call | solution.py:637
Async XLA Ops:
  0.6 54.8 %copy-start.1 = (bf16[288,320]{1,0:T(8,128)(2,1)S(1)}, bf16[288,320]{1,0:T(8,128)(2,1)}, u32[]{:S(2)}) copy-start(bf16[288,320]{1,0:T(8,128)(2,1)} %constant.17.clone.rows_p) | copy-start | bytes 552964
  55.5 1.3 %copy-start = (bf16[2,2,320,512]{3,2,1,0:T(8,128)(2,1)S(1)}, bf16[2,2,320,512]{3,2,1,0:T(8,128)(2,1)}, u32[]{:S(2)}) copy-start(bf16[2,2,320,512]{3,2,1,0:T(8,128)(2,1)} %get-tuple-element.6.pieces_h) | copy-start | bytes 3932164
  56.8 0.7 %copy-start.2 = (f32[4,512]{1,0:T(4,128)S(1)}, f32[4,512]{1,0:T(4,128)}, u32[]{:S(2)}) copy-start(f32[4,512]{1,0:T(4,128)} %get-tuple-element.7.means_in) | copy-start | bytes 24580

commit v4 on v2

--- a/solution.py
+++ b/solution.py
@@ -14,6 +14,8 @@
 D2 = 1024
 EPS = 1e-05
 MASKED = -1e30
+CELLS = 36
+SENT = 72
 QUAD = 40
 QUADS = 160
 GROUP = 144
@@ -35,18 +37,24 @@
 
 @functools.lru_cache(None)
 def tables(lats, lons):
-    q, l, r, c = grid(4, 2, 3, 6)
-    quads = q * QUAD + l * 18 + r * 6 + c
-    to_quads = permutation(QUADS, GROUP, quads, l * 72 + r * 24 + q * 6 + c)
-    to_window = permutation(GROUP, QUADS, l * 72 + q * 18 + r * 6 + c, quads)
-    ro, co, l, cr, cc = grid(2, 2, 2, 3, 6)
+    q, f, l, r, c = grid(4, 2, 2, 3, 6)
+    token = l * 18 + r * 6 + c
+    quads = q * SENT + f * CELLS + token
+    to_quads = permutation(
+        4 * SENT, 2 * GROUP, quads, f * GROUP + l * 72 + r * 24 + q * 6 + c
+    )
+    window = l * 72 + q * 18 + r * 6 + c
+    to_window = permutation(2 * GROUP, 4 * SENT, f * GROUP + window, quads)
+    to_coarse = permutation(2 * QUADS, 4 * SENT, f * QUADS + q * QUAD + token, quads)
+    coarse_window = permutation(GROUP, QUADS, window[:, 0], (q * QUAD + token)[:, 0])
+    f, ro, co, l, cr, cc = grid(2, 2, 2, 2, 3, 6)
     row, col = 2 * cr + ro, 2 * cc + co
     quad = (row // 3) * 2 + col // 6
     to_patches = permutation(
-        QUADS,
-        QUADS,
-        (2 * ro + co) * QUAD + l * 18 + cr * 6 + cc,
-        quad * QUAD + l * 18 + (row % 3) * 6 + col % 6,
+        2 * QUADS,
+        4 * SENT,
+        f * QUADS + (2 * ro + co) * QUAD + l * 18 + cr * 6 + cc,
+        quad * SENT + f * CELLS + l * 18 + (row % 3) * 6 + col % 6,
     )
     l, row, col = grid(2, 6, 24)
     j, c12 = col // 12, col % 12
@@ -84,8 +92,10 @@
         to_window,
         np.ascontiguousarray(to_window.T),
         to_patches,
+        to_coarse,
+        coarse_window,
+        sums.astype(ml_dtypes.bfloat16),
         to_rows,
-        sums.astype(ml_dtypes.bfloat16),
         scale,
     )
 
@@ -96,6 +106,21 @@
 
 def dot_nt(a, b):
     return lax.dot_general(a, b, (((1,), (1,)), ((), ())), preferred_element_type=F32)
+
+
+def stacked(x):
+    half = x.shape[1] // 2
+    return jnp.concatenate([x[:, :half], x[:, half:]], 0)
+
+
+def unstacked(x):
+    half = x.shape[0] // 2
+    return jnp.concatenate([x[:half], x[half:]], 1)
+
+
+def quad_rows(quads):
+    rows = quads.shape[0] * quads.shape[1] * quads.shape[2]
+    return quads.astype(F32).reshape(rows, quads.shape[3]).astype(BF16)
 
 
 def layer_norm(x, gain):
@@ -120,12 +145,14 @@
     window_h,
     unwindow_h,
     patches_h,
+    to_coarse_h,
+    coarse_window_h,
+    sums_h,
     rows_h,
-    sums_h,
     gain1,
     gainm,
     gain2,
-    decoded,
+    decoded_h,
     means,
     latent,
     triple1,
@@ -138,8 +165,10 @@
     window_p,
     unwindow_p,
     patches_p,
+    to_coarse_p,
+    coarse_window_p,
+    sums,
     rows_p,
-    sums,
     xq,
     fq,
     normed,
@@ -157,9 +186,11 @@
     fg,
     fsum,
     usums,
+    decoded_v,
     part1,
     part2,
     load_sem,
+    out_sem,
     send_sem,
     recv_sem,
     ar_send,
@@ -190,12 +221,15 @@
                 (triple2_h, triple2),
                 (out2_h, out2),
                 (split_h, splitw),
+                (to_coarse_h, to_coarse_p),
+                (coarse_window_h, coarse_window_p),
                 (rows_h, rows_p),
             ]
         )
     ]
     (l_latent, l_quads, l_window, l_triple1, l_unwindow, l_out1, l_sums) = loads[:7]
-    (l_patches, l_merge, l_triple2, l_out2, l_split, l_rows) = loads[7:]
+    (l_patches, l_merge, l_triple2, l_out2, l_split) = loads[7:12]
+    (l_coarse, l_window2, l_rows) = loads[12:]
     for load in loads:
         load.start()
 
@@ -274,8 +308,8 @@
     def form_quads(h):
         def form(qr, carry):
             rows = jnp.concatenate([latent[int(l), qr].astype(F32) for l in LEVELS[h]], 0)
-            quads = dot(quads_p[...], rows.astype(BF16))
-            xq[h, qr, pl.ds(0, 4)] = quads.reshape(4, QUAD, D1).astype(BF16)
+            quads = dot(quads_p[...], stacked(rows.astype(BF16)))
+            xq[h, qr, pl.ds(0, 4)] = quads.reshape(4, SENT, D1 // 2).astype(BF16)
             return carry
 
         lax.fori_loop(0, 4, form, 0, unroll=True)
@@ -364,12 +398,12 @@
         x, kinds = [], []
         for h, a, b in slots:
             quads = xq[h, pl.ds(1 + 2 * a, 2), pl.ds(1 + 2 * b, 2)]
-            x.append(dot(window_p[...], quads.astype(F32).reshape(QUADS, D1).astype(BF16)))
+            x.append(unstacked(dot(window_p[...], quad_rows(quads))))
             kinds.append(h + jnp.where((a == 1) & (lat == lats - 1), 2, 0))
         fine = section(jnp.concatenate(x, 0), gain1[...], triple1, out1, D1, kinds).astype(BF16)
         for slot, (h, a, b) in enumerate(slots):
             own = fine[slot * GROUP : (slot + 1) * GROUP]
-            quads = dot(unwindow_p[...], own).reshape(2, 2, QUAD, D1)
+            quads = dot(unwindow_p[...], stacked(own)).reshape(2, 2, SENT, D1 // 2)
             fq[h, pl.ds(1 + 2 * a, 2), pl.ds(1 + 2 * b, 2)] = quads.astype(BF16)
             fsum[...] += dot(sums[h, a], own)
 
@@ -397,13 +431,14 @@
         b_dia(h).start()
 
     l_patches.wait()
+    l_window2.wait()
     l_merge.wait()
     l_triple2.wait()
     l_out2.wait()
 
     def patches(h, first_r, first_c):
         x = fq[h, pl.ds(first_r, 2), pl.ds(first_c, 2)]
-        return dot(patches_p[...], x.astype(F32).reshape(QUADS, D1).astype(BF16))
+        return unstacked(dot(patches_p[...], quad_rows(x)))
 
     def coarse_half(h, carry):
         f_dia(h).wait_recv()
@@ -420,13 +455,18 @@
         for i in range(4):
             lanes = slice(i * 256, (i + 1) * 256)
             coarse[:, lanes] = dot(groupn[...], mergew[:, lanes]).astype(BF16)
-        x = dot(window_p[...], coarse[...])
+        x = dot(coarse_window_p[...], coarse[...])
         kind = h + jnp.where(lat == lats - 1, 2, 0)
         upper = section(x, gain2[...], triple2, out2, D2, [kind]).astype(BF16)
-        up[h] = dot(unwindow_p[...], upper).reshape(2, 2, QUAD, D2).astype(BF16)
-        u_lon(h).start()
-        u_lat(h).start()
-        u_dia(h).start()
+        quads = dot(unwindow_p[...], stacked(upper))
+        up[h] = quads.reshape(2, 2, SENT, D2 // 2).astype(BF16)
+
+        @pl.when(h == 0)
+        def _():
+            u_lon(0).start()
+            u_lat(0).start()
+            u_dia(0).start()
+
         ur[h, 1, 1] = up[h, 0, 0]
         usums[...] += dot(sums[h, 2], upper)
         return carry
@@ -460,6 +500,9 @@
     ar2 = [ar_copy(part2, lon, lats + k, at(0, k)) for k in range(1, lons)]
     for c in ar1:
         c.start()
+    u_lon(1).start()
+    u_lat(1).start()
+    u_dia(1).start()
 
     def skip(h):
         b_lat(h).wait_recv()
@@ -471,11 +514,16 @@
                 rows = slice(cq * QUAD, (cq + 1) * QUAD)
                 fg[h, off, rows, :] = x[off * QUAD : (off + 1) * QUAD]
 
+    def out_copy(level, i):
+        return pltpu.make_async_copy(
+            decoded_v.at[level, i], decoded_h.at[level, i], out_sem.at[2 * level + i]
+        )
+
     def split(h):
         u_lat(h).wait_recv()
         u_lon(h).wait_recv()
         u_dia(h).wait_recv()
-        ub[...] = ur[h].astype(F32).reshape(QUADS, D2).astype(BF16)
+        ub[...] = unstacked(dot(to_coarse_p[...], quad_rows(ur[h]))).astype(BF16)
         for i in range(8):
             dst = slice((i % 2) * 256, (i % 2) * 256 + 256)
             fg[h, i // 2, :, dst] += dot(ub[...], splitw[:, i * 256 : (i + 1) * 256])
@@ -484,12 +532,14 @@
             for j in range(2):
                 rows = slice((2 * i + j) * QUAD, (2 * i + j + 1) * QUAD)
                 pieces += [fg[h, off, rows, :] for off in range(4)]
-            x = jnp.concatenate(pieces, 0).astype(BF16)
-            x = dot(rows_p[...], x).astype(BF16)
+            x = dot(rows_p[...], jnp.concatenate(pieces, 0).astype(BF16)).astype(BF16)
             for l in range(2):
-                decoded[int(LEVELS[h][l]), i] = x[l * 144 : (l + 1) * 144]
+                level = int(LEVELS[h][l])
+                decoded_v[level, i] = x[l * 144 : (l + 1) * 144]
+                out_copy(level, i).start()
 
     skip(0)
+    l_coarse.wait()
     l_rows.wait()
     split(0)
     for c in ar1:
@@ -512,8 +562,23 @@
     for c in (x_lat, x_lon, x_dia, f_lat, f_lon, f_dia, b_lat, b_lon, b_dia, u_lat, u_lon, u_dia):
         c(0).wait_send()
         c(1).wait_send()
+    for level in range(4):
+        for i in range(2):
+            out_copy(level, i).wait()
     for c in ar1 + ar2:
         c.wait_send()
+
+
+def hand_on(decoded_in, means_in, decoded, means, sems):
+    copies = [
+        pltpu.make_async_copy(decoded_in.at[level], decoded.at[level], sems.at[level])
+        for level in range(4)
+    ]
+    for copy in copies:
+        copy.start()
+    means[...] = means_in[...]
+    for copy in copies:
+        copy.wait()
 
 
 def solution(mesh):
@@ -543,8 +608,8 @@
                 jax.ShapeDtypeStruct((4, 2, 144, D1), BF16),
                 jax.ShapeDtypeStruct((4, D1), F32),
             ),
-            in_specs=[hbm] * 13 + [vmem] * 3,
-            out_specs=(vmem, vmem),
+            in_specs=[hbm] * 15 + [vmem] * 3,
+            out_specs=(hbm, vmem),
             scratch_shapes=[
                 bf(4, 4, 72, D1),
                 bf(D1, 3 * D1),
@@ -553,14 +618,16 @@
                 bf(D2, 3 * D2),
                 bf(D2, D2),
                 bf(D2, 4 * D1),
-                bf(QUADS, GROUP),
+                bf(4 * SENT, 2 * GROUP),
+                bf(2 * GROUP, 4 * SENT),
+                bf(4 * SENT, 2 * GROUP),
+                bf(2 * QUADS, 4 * SENT),
+                bf(2 * QUADS, 4 * SENT),
                 bf(GROUP, QUADS),
-                bf(QUADS, GROUP),
-                bf(QUADS, QUADS),
+                bf(2, 3, 16, GROUP),
                 bf(2 * GROUP, 2 * QUADS),
-                bf(2, 3, 16, GROUP),
-                bf(2, 5, 5, QUAD, D1),
-                bf(2, 6, 6, QUAD, D1),
+                bf(2, 5, 5, SENT, D1 // 2),
+                bf(2, 6, 6, SENT, D1 // 2),
                 bf(2 * GROUP, D2),
                 bf(2 * GROUP, D2),
                 bf(2 * GROUP, D2),
@@ -570,15 +637,17 @@
                 f4(QUADS, 4 * D1),
                 bf(QUADS, 4 * D1),
                 bf(QUADS, D2),
-                bf(2, 2, 2, QUAD, D2),
-                bf(2, 2, 2, QUAD, D2),
+                bf(2, 2, 2, SENT, D2 // 2),
+                bf(2, 2, 2, SENT, D2 // 2),
                 bf(QUADS, D2),
                 f4(2, 4, QUADS, D1),
                 f4(16, D1),
                 f4(16, D2),
+                bf(4, 2, 144, D1),
                 f4(lats, 4, D1),
                 f4(lons, 4, D1),
-                pltpu.SemaphoreType.DMA((13,)),
+                pltpu.SemaphoreType.DMA((15,)),
+                pltpu.SemaphoreType.DMA((8,)),
                 pltpu.SemaphoreType.DMA((24,)),
                 pltpu.SemaphoreType.DMA((24,)),
                 pltpu.SemaphoreType.DMA((lats + lons,)),
@@ -600,6 +669,17 @@
             gain_merge.reshape(1, -1),
             gain_second.reshape(1, -1),
         )
+        decoded, means = pl.pallas_call(
+            hand_on,
+            name="hand_on",
+            out_shape=(
+                jax.ShapeDtypeStruct((4, 2, 144, D1), BF16),
+                jax.ShapeDtypeStruct((4, D1), F32),
+            ),
+            in_specs=[pl.BlockSpec(memory_space=pltpu.HBM), vmem],
+            out_specs=(pl.BlockSpec(memory_space=pltpu.HBM), vmem),
+            scratch_shapes=[pltpu.SemaphoreType.DMA((4,))],
+        )(decoded, means)
         return decoded.reshape(4, 12, 24, D1), means
 
     in_specs = (P(None, "lat", "lon", None),) + (P(),) * 9

time: 60.5 us -> 91.1 us (1.51)
  Pallas kernels: 56.7 us -> 90.2 us
  local copies, waits for them, and re-layouts: 2.99 us -> 0 us
    pallas_call x0 -> x1, Pallas kernels: none -> 38.2 us  [shards(): pl.pallas_call(hand_on, name='hand_on', out_shape=(jax.ShapeDtypeStruct((...]
    pallas_call x1, Pallas kernels: 56.7 us -> 52.1 us  [shards(): pl.pallas_call(functools.partial(kernel, lats, lons, scale), name='window...]
    unnamed x4 -> x0, local copies, waits for them, and re-layouts: 2.99 us -> none
where the time goes in v4:
time: 91.1 us; the launch traced here: 90.9 us
  Pallas kernels  90.2 us (99%)
    pallas_call x1, Pallas kernels, shards(): pl.pallas_call(functools.partial(kernel, lats, lons, scale), name='window...  52.1 us
    pallas_call x1, Pallas kernels, shards(): pl.pallas_call(hand_on, name='hand_on', out_shape=(jax.ShapeDtypeStruct((...  38.2 us

profile of v4, /device:TPU:1, one launch (start us, length us, event | category | flops | bytes accessed | tf_op | source)
XLA Modules:
  0.0 90.9 jit_solution(5520933314449651238)
XLA Ops:
  0.6 52.1 %windows.1 = (bf16[4,2,144,512]{3,2,1,0:T(8,128)(2,1)}, f32[4,512]{1,0:T(4,128)}) custom-call(bf16[4,4,72,512]{3,2,1,0:T(8,128)(2,1)} %bitcast.5, bf16[512,1536]{1,0:T(8,128)(2,1)} %triple1_h.1, bf16[512,512]{1,0:T(8,128)(2,1)} %out1_h.1, bf16[2048,1024]{1,0:T(8,128)(2,1)} %merge_h.1, bf16[1024,3072]{1,0:T(8,128)(2,1)} %triple2_h.1, ...), custom_call_target="tpu_custom_call" | custom-call | tf_op jit(solution)/shard_map/windows/pallas_call | solution.py:604
  52.7 38.2 %hand_on.1 = (bf16[4,2,144,512]{3,2,1,0:T(8,128)(2,1)}, f32[4,512]{1,0:T(4,128)}) custom-call(bf16[4,2,144,512]{3,2,1,0:T(8,128)(2,1)} %get-tuple-element.6.decoded_in, f32[4,512]{1,0:T(4,128)} %get-tuple-element.7.means_in), custom_call_target="tpu_custom_call" | custom-call | tf_op jit(solution)/shard_map/hand_on/pallas_call | solution.py:672

commit v5 on v4

--- a/solution.py
+++ b/solution.py
@@ -320,9 +320,6 @@
     x_lat(0).start()
     x_dia(0).start()
     form_quads(1)
-    x_lon(1).start()
-    x_lat(1).start()
-    x_dia(1).start()
 
     l_window.wait()
     l_triple1.wait()
@@ -382,6 +379,12 @@
 
         @pl.when(w == 1)
         def _():
+            x_lon(0).wait_send()
+            x_lat(0).wait_send()
+            x_dia(0).wait_send()
+            x_lon(1).start()
+            x_lat(1).start()
+            x_dia(1).start()
             x_lon(0).wait_recv()
             x_lat(0).wait_recv()
 
@@ -559,7 +562,9 @@
     for k in range(1, lons):
         total += part2[k]
     means[...] = total * (1.0 / scale)
-    for c in (x_lat, x_lon, x_dia, f_lat, f_lon, f_dia, b_lat, b_lon, b_dia, u_lat, u_lon, u_dia):
+    for c in (x_lat, x_lon, x_dia):
+        c(1).wait_send()
+    for c in (f_lat, f_lon, f_dia, b_lat, b_lon, b_dia, u_lat, u_lon, u_dia):
         c(0).wait_send()
         c(1).wait_send()
     for level in range(4):
@@ -567,18 +572,6 @@
             out_copy(level, i).wait()
     for c in ar1 + ar2:
         c.wait_send()
-
-
-def hand_on(decoded_in, means_in, decoded, means, sems):
-    copies = [
-        pltpu.make_async_copy(decoded_in.at[level], decoded.at[level], sems.at[level])
-        for level in range(4)
-    ]
-    for copy in copies:
-        copy.start()
-    means[...] = means_in[...]
-    for copy in copies:
-        copy.wait()
 
 
 def solution(mesh):
@@ -669,17 +662,6 @@
             gain_merge.reshape(1, -1),
             gain_second.reshape(1, -1),
         )
-        decoded, means = pl.pallas_call(
-            hand_on,
-            name="hand_on",
-            out_shape=(
-                jax.ShapeDtypeStruct((4, 2, 144, D1), BF16),
-                jax.ShapeDtypeStruct((4, D1), F32),
-            ),
-            in_specs=[pl.BlockSpec(memory_space=pltpu.HBM), vmem],
-            out_specs=(pl.BlockSpec(memory_space=pltpu.HBM), vmem),
-            scratch_shapes=[pltpu.SemaphoreType.DMA((4,))],
-        )(decoded, means)
         return decoded.reshape(4, 12, 24, D1), means
 
     in_specs = (P(None, "lat", "lon", None),) + (P(),) * 9

time: 91.1 us -> 55.7 us (0.61)
  Pallas kernels: 90.2 us -> 51.8 us
  local copies, waits for them, and re-layouts: 0 us -> 2.99 us
    pallas_call x1 -> x0, Pallas kernels: 38.2 us -> none  [shards(): pl.pallas_call(hand_on, name='hand_on', out_shape=(jax.ShapeDtypeStruct((...]
    unnamed x0 -> x4, local copies, waits for them, and re-layouts: none -> 2.99 us
where the time goes in v5:
time: 55.7 us; the launch traced here: 55.5 us
  Pallas kernels  51.8 us (93%)
  local copies, waits for them, and re-layouts  2.99 us (5%)
  between operations  0.65 us (1%)
    pallas_call x1, Pallas kernels, shards(): pl.pallas_call(functools.partial(kernel, lats, lons, scale), name='window...  51.8 us
    unnamed x4, local copies, waits for them, and re-layouts  2.99 us

profile of v5, /device:TPU:1, one launch (start us, length us, event | category | flops | bytes accessed | tf_op | source)
XLA Modules:
  0.0 55.5 jit_solution(13641915818726033276)
XLA Ops:
  0.6 51.8 %windows.1 = (bf16[4,2,144,512]{3,2,1,0:T(8,128)(2,1)}, f32[4,512]{1,0:T(4,128)}) custom-call(bf16[4,4,72,512]{3,2,1,0:T(8,128)(2,1)} %bitcast.6, bf16[512,1536]{1,0:T(8,128)(2,1)} %triple1_h.1, bf16[512,512]{1,0:T(8,128)(2,1)} %out1_h.1, bf16[2048,1024]{1,0:T(8,128)(2,1)} %merge_h.1, bf16[1024,3072]{1,0:T(8,128)(2,1)} %triple2_h.1, ...), custom_call_target="tpu_custom_call" | custom-call | tf_op jit(solution)/shard_map/windows/pallas_call | solution.py:597
  52.5 0.0 copy-start
  52.5 2.4 %copy.22 = bf16[4,12,24,512]{3,2,1,0:T(8,128)(2,1)} copy(bf16[4,12,24,512]{3,2,1,0:T(8,128)(2,1)} %bitcast.5) | data formatting | bytes 2359296
  54.9 0.0 copy-done
  54.9 0.6 %copy.23 = f32[4,512]{1,0:T(4,128)} copy(f32[4,512]{1,0:T(4,128)S(1)} %copy-done) | data formatting | bytes 16384
Async XLA Ops:
  52.5 2.4 %copy-start = (f32[4,512]{1,0:T(4,128)S(1)}, f32[4,512]{1,0:T(4,128)}, u32[]{:S(2)}) copy-start(f32[4,512]{1,0:T(4,128)} %get-tuple-element.9) | copy-start | bytes 24580

commit v6 on v5

--- a/solution.py
+++ b/solution.py
@@ -187,8 +187,8 @@
     fsum,
     usums,
     decoded_v,
+    part2,
     part1,
-    part2,
     load_sem,
     out_sem,
     send_sem,
@@ -204,6 +204,12 @@
             "lat": lax.rem(lat + dlat + lats, lats),
             "lon": lax.rem(lon + dlon + lons, lons),
         }
+
+    barrier = pltpu.get_barrier_semaphore()
+    peers = [at(k, 0) for k in range(1, lats)] + [at(0, k) for k in range(1, lons)]
+    peers += [at(1, 1), at(-1, -1)]
+    for peer in peers:
+        pl.semaphore_signal(barrier, inc=1, device_id=peer, device_id_type=MESH)
 
     loads = [
         pltpu.make_async_copy(s, d, load_sem.at[i])
@@ -230,14 +236,8 @@
     (l_latent, l_quads, l_window, l_triple1, l_unwindow, l_out1, l_sums) = loads[:7]
     (l_patches, l_merge, l_triple2, l_out2, l_split) = loads[7:12]
     (l_coarse, l_window2, l_rows) = loads[12:]
-    for load in loads:
+    for load in loads[:7]:
         load.start()
-
-    barrier = pltpu.get_barrier_semaphore()
-    peers = [at(k, 0) for k in range(1, lats)] + [at(0, k) for k in range(1, lons)]
-    peers += [at(1, 1), at(-1, -1)]
-    for peer in peers:
-        pl.semaphore_signal(barrier, inc=1, device_id=peer, device_id_type=MESH)
 
     tq = lax.broadcasted_iota(jnp.int32, (GROUP, GROUP), 0)
     tk = lax.broadcasted_iota(jnp.int32, (GROUP, GROUP), 1)
@@ -315,6 +315,8 @@
         lax.fori_loop(0, 4, form, 0, unroll=True)
 
     form_quads(0)
+    for load in loads[7:]:
+        load.start()
     pl.semaphore_wait(barrier, len(peers))
     x_lon(0).start()
     x_lat(0).start()
@@ -487,7 +489,7 @@
             t = dot(usum, splitw[:, off * D1 : (off + 1) * D1])
             t = t[:8] + t[8:]
             partial += t[4 * ro : 4 * ro + 4]
-    part1[lat] = partial
+    part1[lon] = partial
 
     def ar_copy(buf, me, number, target):
         return pltpu.make_async_remote_copy(
@@ -499,8 +501,8 @@
             device_id_type=MESH,
         )
 
-    ar1 = [ar_copy(part1, lat, k, at(k, 0)) for k in range(1, lats)]
-    ar2 = [ar_copy(part2, lon, lats + k, at(0, k)) for k in range(1, lons)]
+    ar2 = [ar_copy(part2, lat, k, at(k, 0)) for k in range(1, lats)]
+    ar1 = [ar_copy(part1, lon, lats + k, at(0, k)) for k in range(1, lons)]
     for c in ar1:
         c.start()
     u_lon(1).start()
@@ -542,24 +544,24 @@
                 out_copy(level, i).start()
 
     skip(0)
+    skip(1)
     l_coarse.wait()
     l_rows.wait()
     split(0)
     for c in ar1:
         c.wait_recv()
     total = part1[0]
-    for k in range(1, lats):
+    for k in range(1, lons):
         total += part1[k]
-    part2[lon] = total
+    part2[lat] = total
     for c in ar2:
         c.start()
-    skip(1)
     split(1)
 
     for c in ar2:
         c.wait_recv()
     total = part2[0]
-    for k in range(1, lons):
+    for k in range(1, lats):
         total += part2[k]
     means[...] = total * (1.0 / scale)
     for c in (x_lat, x_lon, x_dia):
@@ -570,7 +572,7 @@
     for level in range(4):
         for i in range(2):
             out_copy(level, i).wait()
-    for c in ar1 + ar2:
+    for c in ar2 + ar1:
         c.wait_send()
 
 

time: 55.7 us -> 54.2 us (0.973)
  Pallas kernels: 51.8 us -> 50.3 us
    pallas_call x1, Pallas kernels: 51.8 us -> 50.3 us  [shards(): pl.pallas_call(functools.partial(kernel, lats, lons, scale), name='window...]
where the time goes in v6:
time: 54.2 us; the launch traced here: 54 us
  Pallas kernels  50.3 us (93%)
  local copies, waits for them, and re-layouts  2.99 us (6%)
  between operations  0.65 us (1%)
    pallas_call x1, Pallas kernels, shards(): pl.pallas_call(functools.partial(kernel, lats, lons, scale), name='window...  50.3 us
    unnamed x4, local copies, waits for them, and re-layouts  2.99 us

profile of v6, /device:TPU:1, one launch (start us, length us, event | category | flops | bytes accessed | tf_op | source)
XLA Modules:
  0.0 54.0 jit_solution(7093132074649273400)
XLA Ops:
  0.6 50.3 %windows.1 = (bf16[4,2,144,512]{3,2,1,0:T(8,128)(2,1)}, f32[4,512]{1,0:T(4,128)}) custom-call(bf16[4,4,72,512]{3,2,1,0:T(8,128)(2,1)} %bitcast.6, bf16[512,1536]{1,0:T(8,128)(2,1)} %triple1_h.1, bf16[512,512]{1,0:T(8,128)(2,1)} %out1_h.1, bf16[2048,1024]{1,0:T(8,128)(2,1)} %merge_h.1, bf16[1024,3072]{1,0:T(8,128)(2,1)} %triple2_h.1, ...), custom_call_target="tpu_custom_call" | custom-call | tf_op jit(solution)/shard_map/windows/pallas_call | solution.py:599
  51.0 0.0 copy-start
  51.0 2.4 %copy.22 = bf16[4,12,24,512]{3,2,1,0:T(8,128)(2,1)} copy(bf16[4,12,24,512]{3,2,1,0:T(8,128)(2,1)} %bitcast.5) | data formatting | bytes 2359296
  53.4 0.0 copy-done
  53.4 0.6 %copy.23 = f32[4,512]{1,0:T(4,128)} copy(f32[4,512]{1,0:T(4,128)S(1)} %copy-done) | data formatting | bytes 16384
Async XLA Ops:
  51.0 2.4 %copy-start = (f32[4,512]{1,0:T(4,128)S(1)}, f32[4,512]{1,0:T(4,128)}, u32[]{:S(2)}) copy-start(f32[4,512]{1,0:T(4,128)} %get-tuple-element.9) | copy-start | bytes 24580

commit v7 on v6

--- a/solution.py
+++ b/solution.py
@@ -547,7 +547,6 @@
     skip(1)
     l_coarse.wait()
     l_rows.wait()
-    split(0)
     for c in ar1:
         c.wait_recv()
     total = part1[0]
@@ -556,6 +555,7 @@
     part2[lat] = total
     for c in ar2:
         c.start()
+    split(0)
     split(1)
 
     for c in ar2:

time: 54.2 us -> 53.7 us (level)
  no operation moved by 1% of the time
where the time goes in v7:
time: 53.7 us; the launch traced here: 53.5 us
  Pallas kernels  49.9 us (93%)
  local copies, waits for them, and re-layouts  2.99 us (6%)
  between operations  0.65 us (1%)
    pallas_call x1, Pallas kernels, shards(): pl.pallas_call(functools.partial(kernel, lats, lons, scale), name='window...  49.9 us
    unnamed x4, local copies, waits for them, and re-layouts  2.99 us

profile of v7, /device:TPU:1, one launch (start us, length us, event | category | flops | bytes accessed | tf_op | source)
XLA Modules:
  0.0 53.5 jit_solution(5564034614374205193)
XLA Ops:
  0.6 49.9 %windows.1 = (bf16[4,2,144,512]{3,2,1,0:T(8,128)(2,1)}, f32[4,512]{1,0:T(4,128)}) custom-call(bf16[4,4,72,512]{3,2,1,0:T(8,128)(2,1)} %bitcast.6, bf16[512,1536]{1,0:T(8,128)(2,1)} %triple1_h.1, bf16[512,512]{1,0:T(8,128)(2,1)} %out1_h.1, bf16[2048,1024]{1,0:T(8,128)(2,1)} %merge_h.1, bf16[1024,3072]{1,0:T(8,128)(2,1)} %triple2_h.1, ...), custom_call_target="tpu_custom_call" | custom-call | tf_op jit(solution)/shard_map/windows/pallas_call | solution.py:599
  50.5 0.0 copy-start
  50.5 2.4 %copy.22 = bf16[4,12,24,512]{3,2,1,0:T(8,128)(2,1)} copy(bf16[4,12,24,512]{3,2,1,0:T(8,128)(2,1)} %bitcast.5) | data formatting | bytes 2359296
  52.9 0.0 copy-done
  52.9 0.6 %copy.23 = f32[4,512]{1,0:T(4,128)} copy(f32[4,512]{1,0:T(4,128)S(1)} %copy-done) | data formatting | bytes 16384
Async XLA Ops:
  50.5 2.4 %copy-start = (f32[4,512]{1,0:T(4,128)S(1)}, f32[4,512]{1,0:T(4,128)}, u32[]{:S(2)}) copy-start(f32[4,512]{1,0:T(4,128)} %get-tuple-element.9) | copy-start | bytes 24580

commit v8 on v7

--- a/solution.py
+++ b/solution.py
@@ -445,6 +445,18 @@
         x = fq[h, pl.ds(first_r, 2), pl.ds(first_c, 2)]
         return unstacked(dot(patches_p[...], quad_rows(x)))
 
+    def ar_copy(buf, me, number, target):
+        return pltpu.make_async_remote_copy(
+            src_ref=buf.at[me],
+            dst_ref=buf.at[me],
+            send_sem=ar_send.at[number],
+            recv_sem=ar_recv.at[number],
+            device_id=target,
+            device_id_type=MESH,
+        )
+
+    ar2 = [ar_copy(part2, lat, k, at(k, 0)) for k in range(1, lats)]
+    ar1 = [ar_copy(part1, lon, lats + k, at(0, k)) for k in range(1, lons)]
     def coarse_half(h, carry):
         f_dia(h).wait_recv()
         f_lat(h).wait_recv()
@@ -463,51 +475,34 @@
         x = dot(coarse_window_p[...], coarse[...])
         kind = h + jnp.where(lat == lats - 1, 2, 0)
         upper = section(x, gain2[...], triple2, out2, D2, [kind]).astype(BF16)
+        usums[...] += dot(sums[h, 2], upper)
+
+        @pl.when(h == 1)
+        def _():
+            usum = usums[:8] + usums[8:]
+            high = usum.astype(BF16).astype(F32)
+            usum = jnp.concatenate([high, usum - high], 0).astype(BF16)
+            l_split.wait()
+            partial = fsum[0:4] + fsum[4:8]
+            for ro in range(2):
+                for co in range(2):
+                    off = 2 * ro + co
+                    t = dot(usum, splitw[:, off * D1 : (off + 1) * D1])
+                    t = t[:8] + t[8:]
+                    partial += t[4 * ro : 4 * ro + 4]
+            part1[lon] = partial
+            for c in ar1:
+                c.start()
+
         quads = dot(unwindow_p[...], stacked(upper))
         up[h] = quads.reshape(2, 2, SENT, D2 // 2).astype(BF16)
-
-        @pl.when(h == 0)
-        def _():
-            u_lon(0).start()
-            u_lat(0).start()
-            u_dia(0).start()
-
+        u_lon(h).start()
+        u_lat(h).start()
+        u_dia(h).start()
         ur[h, 1, 1] = up[h, 0, 0]
-        usums[...] += dot(sums[h, 2], upper)
         return carry
 
     lax.fori_loop(0, 2, coarse_half, 0)
-
-    usum = usums[:8] + usums[8:]
-    high = usum.astype(BF16).astype(F32)
-    usum = jnp.concatenate([high, usum - high], 0).astype(BF16)
-    l_split.wait()
-    partial = fsum[0:4] + fsum[4:8]
-    for ro in range(2):
-        for co in range(2):
-            off = 2 * ro + co
-            t = dot(usum, splitw[:, off * D1 : (off + 1) * D1])
-            t = t[:8] + t[8:]
-            partial += t[4 * ro : 4 * ro + 4]
-    part1[lon] = partial
-
-    def ar_copy(buf, me, number, target):
-        return pltpu.make_async_remote_copy(
-            src_ref=buf.at[me],
-            dst_ref=buf.at[me],
-            send_sem=ar_send.at[number],
-            recv_sem=ar_recv.at[number],
-            device_id=target,
-            device_id_type=MESH,
-        )
-
-    ar2 = [ar_copy(part2, lat, k, at(k, 0)) for k in range(1, lats)]
-    ar1 = [ar_copy(part1, lon, lats + k, at(0, k)) for k in range(1, lons)]
-    for c in ar1:
-        c.start()
-    u_lon(1).start()
-    u_lat(1).start()
-    u_dia(1).start()
 
     def skip(h):
         b_lat(h).wait_recv()

time: 53.7 us -> 53.5 us (level)
  no operation moved by 1% of the time
where the time goes in v8:
time: 53.5 us; the launch traced here: 53.4 us
  Pallas kernels  49.7 us (93%)
  local copies, waits for them, and re-layouts  2.99 us (6%)
  between operations  0.65 us (1%)
    pallas_call x1, Pallas kernels, shards(): pl.pallas_call(functools.partial(kernel, lats, lons, scale), name='window...  49.7 us
    unnamed x4, local copies, waits for them, and re-layouts  2.99 us

profile of v8, /device:TPU:1, one launch (start us, length us, event | category | flops | bytes accessed | tf_op | source)
XLA Modules:
  0.0 53.4 jit_solution(18057199960766840268)
XLA Ops:
  0.6 49.7 %windows.1 = (bf16[4,2,144,512]{3,2,1,0:T(8,128)(2,1)}, f32[4,512]{1,0:T(4,128)}) custom-call(bf16[4,4,72,512]{3,2,1,0:T(8,128)(2,1)} %bitcast.6, bf16[512,1536]{1,0:T(8,128)(2,1)} %triple1_h.1, bf16[512,512]{1,0:T(8,128)(2,1)} %out1_h.1, bf16[2048,1024]{1,0:T(8,128)(2,1)} %merge_h.1, bf16[1024,3072]{1,0:T(8,128)(2,1)} %triple2_h.1, ...), custom_call_target="tpu_custom_call" | custom-call | tf_op jit(solution)/shard_map/windows/pallas_call | solution.py:594
  50.4 0.0 copy-start
  50.4 2.4 %copy.22 = bf16[4,12,24,512]{3,2,1,0:T(8,128)(2,1)} copy(bf16[4,12,24,512]{3,2,1,0:T(8,128)(2,1)} %bitcast.5) | data formatting | bytes 2359296
  52.8 0.0 copy-done
  52.8 0.6 %copy.23 = f32[4,512]{1,0:T(4,128)} copy(f32[4,512]{1,0:T(4,128)S(1)} %copy-done) | data formatting | bytes 16384
Async XLA Ops:
  50.4 2.4 %copy-start = (f32[4,512]{1,0:T(4,128)S(1)}, f32[4,512]{1,0:T(4,128)}, u32[]{:S(2)}) copy-start(f32[4,512]{1,0:T(4,128)} %get-tuple-element.9) | copy-start | bytes 24580
